TPU v7x, 512 devices: a whole 4x4x16 slice. The times are simulated.
512 devices in a mesh: dp: 16 (over z_hi, x, core), blk: 32 (over y, z_lo).
Axes of the slice: x: 4, y: 4, z: 16 (z_hi: 2, z_lo: 8; z = z_hi * 8 + z_lo), core: 2. Of those that a mesh axis runs over, the one named last changes fastest.
Arguments:
- policy_context: bfloat16 [16384, 4096], P('dp', 'blk'), may hold values from -6 to 6
- frozen_context: bfloat16 [16384, 4096], P('dp', 'blk'), may hold values from -6 to 6
- policy_stream: bfloat16 [4608, 16384], P('blk', 'dp'), may hold values from -6 to 6
- frozen_stream: bfloat16 [4608, 16384], P('blk', 'dp'), may hold values from -6 to 6
- targets: bfloat16 [4608, 16384], P('blk', 'dp'), may hold values from -0.09375 to 0.09375
- policy_gain: float32 [4608], P('blk'), may hold values from 0.1 to 1.9
- frozen_gain: float32 [4608], P('blk'), may hold values from 0.1 to 1.9
- policy_weight: bfloat16 [4608, 4096], P('blk'), may hold values from -0.09375 to 0.09375
- frozen_weight: bfloat16 [4608, 4096], P('blk'), may hold values from -0.09375 to 0.09375
- valid_lengths: int32 [256], P('dp'), may hold values from 16 to 64, as said below
- pair_rows: int32 [128, 2], replicated, may hold values from 0 to 255, as said below
Outputs:
- weight_grad: float32 [4608, 4096], P('blk', 'dp')
- margins: float32 [128], replicated
- loss: float32 [], replicated
Inputs may be any that keep to these rules, and one draw needn't show every extreme that they name: `valid_lengths`: at least one sequence has length 64. `pair_rows`: every sequence appears in exactly one pair, as chosen or as rejected.
All inputs are finite; a program needn't handle non-finite values.
Results may differ from a plain program's by a relative error of at most 0.0029.
Values may be sent and summed in bfloat16 or wider, within the bound.
No kernel may reach another device: no remote copies, remote signals or barrier semaphores. Data moves between devices by JAX's collectives and lax.ppermute only.
A program may use at most 64 MiB of HBM per device.

v0:
```python
import jax
import jax.numpy as jnp
from jax import lax
from jax.sharding import PartitionSpec as P

D = 4608


beta_scale = 0.1
epsilon = 1e-06


def slab_product(weight, piece):
    return lax.dot_general(
        weight, piece, (((1,), (1,)), ((), ())), preferred_element_type=jnp.float32
    )


def shards(
    policy_context,
    frozen_context,
    policy_stream,
    frozen_stream,
    targets,
    policy_gain,
    frozen_gain,
    policy_weight,
    frozen_weight,
    valid_lengths,
    pair_rows,
):
    tokens_here = policy_stream.shape[1]
    seqs_here = valid_lengths.shape[0]
    seq_len = tokens_here // seqs_here
    whole_policy = lax.all_gather(policy_context, "blk", axis=1, tiled=True)
    policy_product = lax.dot_general(
        policy_weight, whole_policy, (((1,), (1,)), ((), ())), preferred_element_type=jnp.float32
    )
    frozen_product = slab_product(
        frozen_weight, lax.all_gather(frozen_context, "blk", axis=1, tiled=True)
    )
    policy_hidden = policy_stream.astype(jnp.float32) + policy_product
    frozen_hidden = frozen_stream.astype(jnp.float32) + frozen_product
    target_values = targets.astype(jnp.float32)
    policy_weighted = policy_gain[:, None] * target_values
    frozen_weighted = frozen_gain[:, None] * target_values
    policy_square = jnp.sum(policy_hidden * policy_hidden, axis=0)
    frozen_square = jnp.sum(frozen_hidden * frozen_hidden, axis=0)
    policy_square, frozen_square = lax.psum((policy_square, frozen_square), "blk")
    policy_scale = lax.rsqrt(policy_square / D + epsilon)
    frozen_scale = lax.rsqrt(frozen_square / D + epsilon)
    policy_score, frozen_score = lax.psum(
        (
            jnp.sum(policy_hidden * policy_scale[None, :] * policy_weighted, axis=0),
            jnp.sum(frozen_hidden * frozen_scale[None, :] * frozen_weighted, axis=0),
        ),
        "blk",
    )
    policy_dotted = policy_score / policy_scale
    positions = lax.broadcasted_iota(jnp.int32, (seqs_here, seq_len), 1)
    valid = (positions < valid_lengths[:, None]).astype(jnp.float32)
    policy_sums = jnp.sum(policy_score.reshape(seqs_here, seq_len) * valid, axis=1)
    frozen_sums = jnp.sum(frozen_score.reshape(seqs_here, seq_len) * valid, axis=1)
    every_policy, every_frozen = (
        lax.all_gather(policy_sums, "dp", axis=0, tiled=True),
        lax.all_gather(frozen_sums, "dp", axis=0, tiled=True),
    )
    total_seqs = every_policy.shape[0]
    pair_count = pair_rows.shape[0]
    row_ids = lax.broadcasted_iota(jnp.int32, (pair_count, total_seqs), 1)
    chosen_onehot = (row_ids == pair_rows[:, 0:1]).astype(jnp.float32)
    rejected_onehot = (row_ids == pair_rows[:, 1:2]).astype(jnp.float32)
    gaps = every_policy - every_frozen
    margins = beta_scale * (
        jnp.sum(chosen_onehot * gaps[None, :], axis=1)
        - jnp.sum(rejected_onehot * gaps[None, :], axis=1)
    )
    loss = jnp.sum(jax.nn.softplus(-margins))
    slopes = -jax.nn.sigmoid(-margins)
    own_ids = lax.axis_index("dp") * seqs_here + lax.broadcasted_iota(jnp.int32, (1, seqs_here), 1)
    own_chosen = (pair_rows[:, 0:1] == own_ids).astype(jnp.float32)
    own_rejected = (pair_rows[:, 1:2] == own_ids).astype(jnp.float32)
    coef = beta_scale * jnp.sum(slopes[:, None] * (own_chosen - own_rejected), axis=0)
    token_coef = (coef[:, None] * valid).reshape(tokens_here)
    step_size = token_coef * policy_scale
    correction = policy_dotted * policy_scale * policy_scale / D
    hidden_grad = (
        step_size[None, :] * (policy_weighted - policy_hidden * correction[None, :])
    ).astype(jnp.bfloat16)
    weight_grad = lax.psum_scatter(
        lax.dot_general(
            whole_policy, hidden_grad, (((0,), (1,)), ((), ())), preferred_element_type=jnp.float32
        ),
        "dp",
        scatter_dimension=0,
        tiled=True,
    ).T
    return (weight_grad, margins, loss)


def solution(mesh):
    placed = (
        P("dp", "blk"),
        P("dp", "blk"),
        P("blk", "dp"),
        P("blk", "dp"),
        P("blk", "dp"),
        P("blk"),
        P("blk"),
        P("blk", None),
        P("blk", None),
        P("dp"),
        P(),
    )
    return jax.shard_map(
        shards, mesh=mesh, in_specs=placed, out_specs=(P("blk", "dp"), P(), P()), check_vma=False
    )
```

profile of v0, /device:TPU:6, one launch (start us, length us, event | category | flops | bytes accessed | tf_op | source)
XLA Modules:
  0.0 1092.5 jit_solution(17063972806101999141)
XLA Ops:
  7.2 0.7 all-gather.5.cloned.1.call-update
  8.0 0.7 all-gather.3.cloned.1.call-update
  8.7 1.3 dynamic-slice
  10.7 0.8 slice_bitcast_fusion.1
  11.4 268.0 %all-gather.5.cloned.1.call-done = bf16[1024,4096]{1,0:T(8,128)(2,1)} async-done(((bf16[1024,128]{1,0:T(8,128)(2,1)}), bf16[1024,4096]{1,0:T(8,128)(2,1)}) %all-gather.5.cloned.1.call-update) | async-done | bytes 8388624 | tf_op jit(solution)/shard_map/all_gather | solution.py:40
  279.4 6.3 multiply_reduce_fusion
  285.7 260.4 %all-gather.3.cloned.1.call-done = bf16[1024,4096]{1,0:T(8,128)(2,1)} async-done(((bf16[1024,128]{1,0:T(8,128)(2,1)}), bf16[1024,4096]{1,0:T(8,128)(2,1)}) %all-gather.3.cloned.1.call-update) | async-done | bytes 8388624 | tf_op jit(solution)/shard_map/all_gather | solution.py:35
  546.1 6.7 multiply_reduce_fusion.1
  552.8 126.2 %all-reduce.3 = (f32[1024]{0:T(1024)S(1)}, f32[1024]{0:T(1024)S(1)}) all-reduce(f32[1024]{0:T(1024)S(1)} %get-tuple-element.21, f32[1024]{0:T(1024)S(1)} %get-tuple-element.23), channel_id=1, replica_groups=mesh['dp'=16,'blk'=32] {'blk'}, use_global_device_ids=true, to_apply=%region_6.0 | all-reduce | flops 2048 | bytes 16384 | tf_op jit(solution)/shard_map/psum | solution.py:49
  679.1 0.3 fusion.6
  679.4 0.1 reshape.46
  679.4 224.7 %all-reduce.2 = (f32[1024]{0:T(1024)S(1)}, f32[16,64]{1,0:T(8,128)S(1)}) all-reduce(f32[1024]{0:T(1024)S(1)} %get-tuple-element.4, f32[16,64]{1,0:T(8,128)S(1)} %reshape.46), channel_id=1, replica_groups=mesh['dp'=16,'blk'=32] {'blk'}, use_global_device_ids=true, to_apply=%region_3.0 | all-reduce | flops 2048 | bytes 16384 | tf_op jit(solution)/shard_map/psum | solution.py:52
  904.2 0.1 reshape.45
  904.2 0.2 select_reduce_fusion.2
  904.4 0.2 dynamic-update-slice.1
  904.7 0.2 dynamic-update-slice
  904.9 48.8 %all-reduce.4 = (f32[256]{0:T(256)S(1)}, f32[256]{0:T(256)S(1)}) all-reduce(f32[256]{0:T(256)S(1)} %dynamic-update-slice, f32[256]{0:T(256)S(1)} %dynamic-update-slice.1), channel_id=1, replica_groups=mesh['dp'=16,'blk'=32] {'dp'}, use_global_device_ids=true, to_apply=%add | all-reduce | flops 512 | bytes 4096
  953.7 0.2 select_reduce_fusion
  953.9 0.6 fusion.13
  954.5 0.2 multiply_reduce_fusion.2
  954.7 0.1 fusion.11
  954.8 0.1 mul.152
  954.9 6.4 convolution_bitcast_fusion
  961.3 124.7 %reduce-scatter.2.cloned.1.call-done = f32[256,144]{0,1:T(8,128)} async-done(((f32[4096,144]{0,1:T(8,128)}), f32[256,144]{0,1:T(8,128)}) %reduce-scatter.2.cloned.1.call-update) | async-done | bytes 147472 | tf_op jit(solution)/shard_map/reduce_scatter | solution.py:90
  (26 shorter events, 0.2 us)
Async XLA Ops:
  7.2 272.3 %copy-start = (bf16[144,4096]{1,0:T(8,128)(2,1)S(1)}, bf16[144,4096]{1,0:T(8,128)(2,1)}, u32[]{:S(2)}) copy-start(bf16[144,4096]{1,0:T(8,128)(2,1)} %param.19) | copy-start | bytes 3538948
  7.2 538.9 %copy-start.2 = (bf16[144,1024]{1,0:T(8,128)(2,1)S(1)}, bf16[144,1024]{1,0:T(8,128)(2,1)}, u32[]{:S(2)}) copy-start(bf16[144,1024]{1,0:T(8,128)(2,1)} %param.13) | copy-start | bytes 884740
  7.2 272.2 %all-gather.5.cloned.1.call-start = ((), (), s32[]{:S(2)}) async-start(), calls=%async_computation.2 | async-start | bytes 8650752 | tf_op jit(solution)/shard_map/all_gather | solution.py:40
  7.9 538.2 %all-gather.3.cloned.1.call-start = ((), (), s32[]{:S(2)}) async-start(), calls=%async_computation.1 | async-start | bytes 8650752 | tf_op jit(solution)/shard_map/all_gather | solution.py:35
  8.7 1077.3 %reduce-scatter.2.cloned.1.call-start = ((), (), s32[]{:S(2)}) async-start(), calls=%async_computation.3 | async-start | bytes 2506752 | tf_op jit(solution)/shard_map/reduce_scatter | solution.py:90
  11.4 667.7 %copy-start.1 = (bf16[144,1024]{1,0:T(8,128)(2,1)S(1)}, bf16[144,1024]{1,0:T(8,128)(2,1)}, u32[]{:S(2)}) copy-start(bf16[144,1024]{1,0:T(8,128)(2,1)} %param.15) | copy-start | bytes 884740
  11.4 667.7 %copy-start.3 = (f32[144]{0:T(256)S(1)}, f32[144]{0:T(256)}, u32[]{:S(2)}) copy-start(f32[144]{0:T(256)} %param.16) | copy-start | bytes 1732
  11.4 667.7 %copy-start.5 = (f32[144]{0:T(256)S(1)}, f32[144]{0:T(256)}, u32[]{:S(2)}) copy-start(f32[144]{0:T(256)} %param.17) | copy-start | bytes 1732
  285.7 618.5 %copy-start.4 = (s32[16]{0:T(128)S(1)}, s32[16]{0:T(128)}, u32[]{:S(2)}) copy-start(s32[16]{0:T(128)} %param.20) | copy-start | bytes 196
  954.5 6.8 copy-start.6
Sparse Core Ops, SparseCore 0:
  10.0 269.3 all-gather.4
  281.4 264.6 all-gather.2
  961.4 124.5 reduce-scatter.1
where the time goes:
time: 1090 us
  waiting for transfers between devices  654 us (60%)
  blocking collectives  400 us (37%)
  matrix products  19.4 us (2%)
  between operations  14.5 us (1%)
    all_gather x1, waiting for transfers between devices, shards(): lax.all_gather(frozen_context, 'blk', axis=1, tiled=True)  268 us
    all_gather x1, waiting for transfers between devices, shards(): whole_policy = lax.all_gather(policy_context, 'blk', axis=1, tiled=True)  260 us
    psum x1, blocking collectives, shards(): lax.psum((jnp.sum(policy_hidden * policy_scale[None, :] * policy_weighted...  225 us
    psum x1, blocking collectives, shards(): lax.psum((policy_square, frozen_square), 'blk')  126 us
    reduce_scatter x1, waiting for transfers between devices, shards(): lax.psum_scatter(lax.dot_general(whole_policy, hidden_grad, (((0,), (1,))...  125 us
    unnamed x1, blocking collectives  48.8 us
  transfers between devices with their start and end apart: 3, of which 3 were waited for; matrix products, arithmetic and copies ran while one was open for 1% of the time, Pallas kernels for 0%

commit v1 on v0

v1 whole, which is shorter than its diff:
```python
import jax
import jax.numpy as jnp
from jax import lax
from jax.sharding import Mesh, PartitionSpec as P

D = 4608
NY = 4
NX = 4

beta_scale = 0.1
epsilon = 1e-06


def spread(value, axes, count):
    return lax.all_to_all(jnp.broadcast_to(value[None], (count,) + value.shape), axes, 0, 0)


def swap(count, bit):
    return [(i, i ^ bit) for i in range(count)]


def contract_part(weight):
    rows, features = weight.shape
    parts = weight.reshape(rows, NY, features // NY).transpose(1, 0, 2)
    return lax.all_to_all(parts, "y", 0, 0)


def hidden_of(weight_part, context_part, stream):
    slots, rows, features = weight_part.shape
    partial = lax.dot_general(
        weight_part.reshape(slots * rows, features),
        context_part,
        (((1,), (1,)), ((), ())),
        preferred_element_type=jnp.float32,
    ).astype(jnp.bfloat16)
    parts = lax.all_to_all(partial.reshape(slots, rows, -1), "y", 0, 0)
    return stream.astype(jnp.float32) + jnp.sum(parts.astype(jnp.float32), axis=0)


def shards(
    policy_context,
    frozen_context,
    policy_stream,
    frozen_stream,
    targets,
    policy_gain,
    frozen_gain,
    policy_weight,
    frozen_weight,
    valid_lengths,
    pair_rows,
):
    rows, tokens_here = policy_stream.shape
    seqs_here = valid_lengths.shape[0]
    seq_len = tokens_here // seqs_here
    z_hi, x, core = lax.axis_index("zh"), lax.axis_index("x"), lax.axis_index("c")

    both = lax.all_gather(
        jnp.concatenate([policy_context, frozen_context], 0), "zl", axis=1, tiled=True
    )
    policy_columns, frozen_columns = both[:tokens_here], both[tokens_here:]
    frozen_part = contract_part(frozen_weight)
    policy_part = contract_part(policy_weight)
    all_targets = spread(targets, "y", NY)
    all_gain = spread(policy_gain, "y", NY)

    frozen_hidden = hidden_of(frozen_part, frozen_columns, frozen_stream)
    policy_hidden = hidden_of(policy_part, policy_columns, policy_stream)
    target_values = targets.astype(jnp.float32)
    policy_weighted = policy_gain[:, None] * target_values
    frozen_weighted = frozen_gain[:, None] * target_values
    stats = jnp.stack(
        [
            jnp.sum(policy_hidden * policy_hidden, axis=0),
            jnp.sum(policy_hidden * policy_weighted, axis=0),
            jnp.sum(frozen_hidden * frozen_hidden, axis=0),
            jnp.sum(frozen_hidden * frozen_weighted, axis=0),
        ]
    )
    stats = jnp.sum(spread(stats, "y", NY), axis=0)
    stats = jnp.sum(spread(stats, "zl", 8), axis=0)
    all_hidden = spread(policy_hidden.astype(jnp.bfloat16), "y", NY)

    policy_scale = lax.rsqrt(stats[0] / D + epsilon)
    frozen_scale = lax.rsqrt(stats[2] / D + epsilon)
    policy_dotted = stats[1]
    gap_of_token = policy_scale * policy_dotted - frozen_scale * stats[3]
    positions = lax.broadcasted_iota(jnp.int32, (seqs_here, seq_len), 1)
    valid = (positions < valid_lengths[:, None]).astype(jnp.float32)
    own_gaps = jnp.sum(gap_of_token.reshape(seqs_here, seq_len) * valid, axis=1)
    gaps = spread(own_gaps, ("zh", "x", "c"), 16).reshape(-1)

    total_seqs = gaps.shape[0]
    pair_count = pair_rows.shape[0]
    row_ids = lax.broadcasted_iota(jnp.int32, (pair_count, total_seqs), 1)
    signs = (row_ids == pair_rows[:, 0:1]).astype(jnp.float32) - (
        row_ids == pair_rows[:, 1:2]
    ).astype(jnp.float32)
    margins = beta_scale * jnp.sum(signs * gaps[None, :], axis=1)
    loss = jnp.sum(jax.nn.softplus(-margins))
    slopes = -jax.nn.sigmoid(-margins)
    own_ids = lax.axis_index(("zh", "x", "c")) * seqs_here + lax.broadcasted_iota(
        jnp.int32, (1, seqs_here), 1
    )
    own_chosen = (pair_rows[:, 0:1] == own_ids).astype(jnp.float32)
    own_rejected = (pair_rows[:, 1:2] == own_ids).astype(jnp.float32)
    coef = beta_scale * jnp.sum(slopes[:, None] * (own_chosen - own_rejected), axis=0)
    token_coef = (coef[:, None] * valid).reshape(tokens_here)
    step_size = token_coef * policy_scale
    correction = policy_dotted * policy_scale * policy_scale / D
    hidden_grad = (
        step_size[None, None, :]
        * (
            all_gain[:, :, None] * all_targets.astype(jnp.float32)
            - all_hidden.astype(jnp.float32) * correction[None, None, :]
        )
    ).astype(jnp.bfloat16)

    grad = lax.dot_general(
        hidden_grad.reshape(NY * rows, tokens_here),
        policy_columns,
        (((1,), (0,)), ((), ())),
        preferred_element_type=jnp.float32,
    )
    grad = grad.reshape(NY * rows, 2, 2, 256)
    other = lax.dynamic_index_in_dim(grad, 1 - core, 2, keepdims=False)
    mine = lax.dynamic_index_in_dim(grad, core, 2, keepdims=False)
    grad = mine + lax.ppermute(other, "c", swap(2, 1))
    grad = grad.reshape(NY * rows, 2, 2, 128).transpose(2, 1, 0, 3).reshape(NX, NY * rows, 128)
    grad = jnp.sum(lax.all_to_all(grad, "x", 0, 0), axis=0)
    grad = lax.all_to_all(grad.reshape(NY, rows, 128), "y", 0, 0).reshape(2, 2, rows, 128)
    other = lax.dynamic_index_in_dim(grad, 1 - z_hi, 0, keepdims=False)
    mine = lax.dynamic_index_in_dim(grad, z_hi, 0, keepdims=False)
    grad = mine + lax.ppermute(other, "zh", swap(2, 1))
    half = x // 2
    other = lax.dynamic_index_in_dim(grad, 1 - half, 0, keepdims=False)
    mine = lax.dynamic_index_in_dim(grad, half, 0, keepdims=False)
    other = lax.ppermute(other, "x", swap(NX, 2))
    first = jnp.where(half == 0, mine, other)
    second = jnp.where(half == 0, other, mine)
    weight_grad = jnp.concatenate([first, second], axis=1)
    return (weight_grad, margins, loss)


def solution(mesh):
    dp, blk = ("zh", "x", "c"), ("y", "zl")
    fine = Mesh(mesh.devices.reshape(2, 4, 2, 4, 8), dp + blk)
    placed = (
        P(dp, blk),
        P(dp, blk),
        P(blk, dp),
        P(blk, dp),
        P(blk, dp),
        P(blk),
        P(blk),
        P(blk, None),
        P(blk, None),
        P(dp),
        P(),
    )
    return jax.shard_map(
        shards, mesh=fine, in_specs=placed, out_specs=(P(blk, dp), P(), P()), check_vma=False
    )
```

time: 1090 us -> 349 us (0.32)
  the two profiles are of different devices: /device:TPU:6 before, /device:TPU:32 now
where the time goes in v1:
time: 349 us; the launch traced here: 348 us
  waiting for transfers between devices  216 us (62%)
  starting transfers between devices  53.9 us (15%)
  blocking collectives  27.5 us (8%)
  local copies, waits for them, and re-layouts  18.1 us (5%)
  between operations  14.4 us (4%)
  matrix products  9.5 us (3%)
  other arithmetic  8.94 us (3%)
    all_gather x1, waiting for transfers between devices, shards(): lax.all_gather(jnp.concatenate([policy_context, frozen_context], 0), 'zl'...  83.3 us
    all_to_all x5, waiting for transfers between devices, spread(): lax.all_to_all(jnp.broadcast_to(value[None], (count,) + value.shape), axe...  55 us
    all_to_all x5, starting transfers between devices, spread(): lax.all_to_all(jnp.broadcast_to(value[None], (count,) + value.shape), axe...  27 us
    all_to_all x2, waiting for transfers between devices, hidden_of(): parts = lax.all_to_all(partial.reshape(slots, rows, -1), 'y', 0, 0)  26.8 us
    ppermute x1, waiting for transfers between devices, shards(): grad = mine + lax.ppermute(other, 'zh', swap(2, 1))  21.3 us
    all_to_all x1, blocking collectives, shards(): grad = jnp.sum(lax.all_to_all(grad, 'x', 0, 0), axis=0)  19.5 us
    all_to_all x2, waiting for transfers between devices, contract_part(): return lax.all_to_all(parts, 'y', 0, 0)  14.2 us
    all_to_all x2, starting transfers between devices, hidden_of(): parts = lax.all_to_all(partial.reshape(slots, rows, -1), 'y', 0, 0)  8.52 us
  transfers between devices with their start and end apart: 14, of which 13 were waited for; matrix products, arithmetic and copies ran while one was open for 6% of the time, Pallas kernels for 0%

profile of v1, /device:TPU:32, one launch (start us, length us, event | category | flops | bytes accessed | tf_op | source)
XLA Modules:
  0.0 348.0 jit_solution(1356645917418803096)
XLA Ops:
  11.5 4.6 %all-to-all-start.2 = ((bf16[4,144,1024]{2,1,0:T(8,128)(2,1)}), bf16[4,144,1024]{2,1,0:T(8,128)(2,1)S(1)}, u32[]{:S(2)}, u32[]{:S(2)}) async-start(bf16[4,144,1024]{2,1,0:T(8,128)(2,1)} %copy.29), calls=%async_computation.2 | async-start | bytes 2359296 | tf_op jit(solution)/shard_map/all_to_all | solution.py:25
  18.4 14.2 %all-to-all-done.2 = bf16[4,144,1024]{2,1,0:T(8,128)(2,1)S(1)} async-done(((bf16[4,144,1024]{2,1,0:T(8,128)(2,1)}), bf16[4,144,1024]{2,1,0:T(8,128)(2,1)S(1)}, u32[]{:S(2)}, u32[]{:S(2)}) %all-to-all-start.2) | async-done | bytes 1179680 | tf_op jit(solution)/shard_map/all_to_all | solution.py:25
  32.6 3.5 %all-to-all-start = ((bf16[4,144,1024]{2,1,0:T(8,128)(2,1)}), bf16[4,144,1024]{2,1,0:T(8,128)(2,1)S(1)}, u32[]{:S(2)}, u32[]{:S(2)}) async-start(bf16[4,144,1024]{2,1,0:T(8,128)(2,1)} %copy.28), calls=%async_computation | async-start | bytes 2359296 | tf_op jit(solution)/shard_map/all_to_all | solution.py:25
  36.2 83.3 %all-gather.2.cloned.1.call-done = bf16[2048,1024]{1,0:T(8,128)(2,1)} async-done(((bf16[2048,128]{1,0:T(8,128)(2,1)}), bf16[2048,1024]{1,0:T(8,128)(2,1)}) %all-gather.2.cloned.1.call-update) | async-done | bytes 4194320 | tf_op jit(solution)/shard_map/all_gather | solution.py:58
  119.4 4.1 %fusion.7 = bf16[1024,576]{0,1:T(8,128)(2,1)} fusion(bf16[576,1024]{1,0:T(8,128)(2,1)S(1)} %bitcast.59, bf16[2048,1024]{1,0:T(8,128)(2,1)} %all-gather.2.cloned.1.call-done), kind=kOutput, calls=%fused_computation.9 | convolution fusion | flops 1208549376 | bytes 4456448 | tf_op jit(solution)/shard_map/dot_general | solution.py:30
  123.5 5.0 %all-to-all-start.3 = ((bf16[4,144,1024]{2,1,0:T(8,128)(2,1)}), bf16[4,144,1024]{2,1,0:T(8,128)(2,1)S(1)}, u32[]{:S(2)}, u32[]{:S(2)}) async-start(bf16[4,144,1024]{2,1,0:T(8,128)(2,1)} %bitcast.11), calls=%async_computation.3 | async-start | bytes 2359296 | tf_op jit(solution)/shard_map/all_to_all | solution.py:36
  128.5 4.0 %fusion.4 = bf16[1024,576]{0,1:T(8,128)(2,1)} fusion(bf16[576,1024]{1,0:T(8,128)(2,1)S(1)} %bitcast.60, bf16[2048,1024]{1,0:T(8,128)(2,1)} %all-gather.2.cloned.1.call-done), kind=kOutput, calls=%fused_computation.8 | convolution fusion | flops 1208549376 | bytes 4456448 | tf_op jit(solution)/shard_map/dot_general | solution.py:30
  132.5 12.0 %all-to-all-done.3 = bf16[4,144,1024]{2,1,0:T(8,128)(2,1)S(1)} async-done(((bf16[4,144,1024]{2,1,0:T(8,128)(2,1)}), bf16[4,144,1024]{2,1,0:T(8,128)(2,1)S(1)}, u32[]{:S(2)}, u32[]{:S(2)}) %all-to-all-start.3) | async-done | bytes 1179680 | tf_op jit(solution)/shard_map/all_to_all | solution.py:36
  144.5 3.5 %all-to-all-start.1 = ((bf16[4,144,1024]{2,1,0:T(8,128)(2,1)}), bf16[4,144,1024]{2,1,0:T(8,128)(2,1)S(1)}, u32[]{:S(2)}, u32[]{:S(2)}) async-start(bf16[4,144,1024]{2,1,0:T(8,128)(2,1)} %bitcast.5), calls=%async_computation.1 | async-start | bytes 2359296 | tf_op jit(solution)/shard_map/all_to_all | solution.py:36
  148.4 14.8 %all-to-all-done.1 = bf16[4,144,1024]{2,1,0:T(8,128)(2,1)S(1)} async-done(((bf16[4,144,1024]{2,1,0:T(8,128)(2,1)}), bf16[4,144,1024]{2,1,0:T(8,128)(2,1)S(1)}, u32[]{:S(2)}, u32[]{:S(2)}) %all-to-all-start.1) | async-done | bytes 1179680 | tf_op jit(solution)/shard_map/all_to_all | solution.py:36
  164.6 8.0 %all_to_all.62 = f32[4,4,1024]{2,1,0:T(4,128)S(1)} all-to-all(f32[4,4,1024]{2,1,0:T(4,128)S(1)} %broadcast_in_dim.12), channel_id=1, replica_groups=mesh['zh'=2,'x'=4,'c'=2,'y'=4,'zl'=8] {'y'}, dimensions={0} | all-to-all | bytes 131072 | tf_op jit(solution)/shard_map/all_to_all | solution.py:15
  173.2 11.4 %all-to-all-start.5 = ((f32[8,4,1024]{2,1,0:T(4,128)}), f32[8,4,1024]{2,1,0:T(4,128)S(1)}, u32[]{:S(2)}, u32[]{:S(2)}) async-start(f32[8,4,1024]{2,1,0:T(4,128)} %broadcast_in_dim.13), calls=%async_computation.5 | async-start | bytes 262144 | tf_op jit(solution)/shard_map/all_to_all | solution.py:15
  184.7 9.6 %all-to-all-done.5 = f32[8,4,1024]{2,1,0:T(4,128)S(1)} async-done(((f32[8,4,1024]{2,1,0:T(4,128)}), f32[8,4,1024]{2,1,0:T(4,128)S(1)}, u32[]{:S(2)}, u32[]{:S(2)}) %all-to-all-start.5) | async-done | bytes 131104 | tf_op jit(solution)/shard_map/all_to_all | solution.py:15
  198.5 4.9 %all-to-all-done.7 = f32[4,1,144]{2,1,0:T(1,128)S(1)} async-done(((f32[4,1,144]{2,1,0:T(1,128)}), f32[4,1,144]{2,1,0:T(1,128)S(1)}, u32[]{:S(2)}, u32[]{:S(2)}) %all-to-all-start.7) | async-done | bytes 2336 | tf_op jit(solution)/shard_map/all_to_all | solution.py:15
  204.0 5.2 %all-to-all-start.6 = ((f32[16,1,16]{2,1,0:T(1,128)}), f32[16,1,16]{2,1,0:T(1,128)S(1)}, u32[]{:S(2)}, u32[]{:S(2)}) async-start(f32[16,1,16]{2,1,0:T(1,128)} %broadcast_in_dim.14), calls=%async_computation.6 | async-start | bytes 16384 | tf_op jit(solution)/shard_map/all_to_all | solution.py:15
  209.2 14.7 %all-to-all-done.6 = f32[16,1,16]{2,1,0:T(1,128)S(1)} async-done(((f32[16,1,16]{2,1,0:T(1,128)}), f32[16,1,16]{2,1,0:T(1,128)S(1)}, u32[]{:S(2)}, u32[]{:S(2)}) %all-to-all-start.6) | async-done | bytes 1056 | tf_op jit(solution)/shard_map/all_to_all | solution.py:15
  225.0 3.7 %all-to-all-start.8 = ((bf16[4,144,1024]{2,1,0:T(8,128)(2,1)}), bf16[4,144,1024]{2,1,0:T(8,128)(2,1)S(1)}, u32[]{:S(2)}, u32[]{:S(2)}) async-start(bf16[4,144,1024]{2,1,0:T(8,128)(2,1)} %broadcast_in_dim.16), calls=%async_computation.8 | async-start | bytes 2359296 | tf_op jit(solution)/shard_map/all_to_all | solution.py:15
  235.2 10.3 %all-to-all-done.8 = bf16[4,144,1024]{2,1,0:T(8,128)(2,1)S(1)} async-done(((bf16[4,144,1024]{2,1,0:T(8,128)(2,1)}), bf16[4,144,1024]{2,1,0:T(8,128)(2,1)S(1)}, u32[]{:S(2)}, u32[]{:S(2)}) %all-to-all-start.8) | async-done | bytes 1179680 | tf_op jit(solution)/shard_map/all_to_all | solution.py:15
  247.6 3.5 %all-to-all-start.9 = ((bf16[4,144,1024]{2,1,0:T(8,128)(2,1)}), bf16[4,144,1024]{2,1,0:T(8,128)(2,1)S(1)}, u32[]{:S(2)}, u32[]{:S(2)}) async-start(bf16[4,144,1024]{2,1,0:T(8,128)(2,1)} %broadcast_in_dim.17), calls=%async_computation.9 | async-start | bytes 2359296 | tf_op jit(solution)/shard_map/all_to_all | solution.py:15
  251.5 15.5 %all-to-all-done.9 = bf16[4,144,1024]{2,1,0:T(8,128)(2,1)S(1)} async-done(((bf16[4,144,1024]{2,1,0:T(8,128)(2,1)}), bf16[4,144,1024]{2,1,0:T(8,128)(2,1)S(1)}, u32[]{:S(2)}, u32[]{:S(2)}) %all-to-all-start.9) | async-done | bytes 1179680 | tf_op jit(solution)/shard_map/all_to_all | solution.py:15
  278.3 19.5 %all_to_all.63 = f32[4,576,128]{2,1,0:T(8,128)S(1)} all-to-all(f32[4,576,128]{2,1,0:T(8,128)S(1)} %bitcast.55), channel_id=1, replica_groups=mesh['zh'=2,'x'=4,'c'=2,'y'=4,'zl'=8] {'x'}, dimensions={0} | all-to-all | bytes 2359296 | tf_op jit(solution)/shard_map/all_to_all | solution.py:130
  302.0 6.8 %all-to-all-done.11 = f32[4,144,128]{2,1,0:T(8,128)S(1)} async-done(((f32[4,144,128]{2,1,0:T(8,128)}), f32[4,144,128]{2,1,0:T(8,128)S(1)}, u32[]{:S(2)}, u32[]{:S(2)}) %all-to-all-start.11) | async-done | bytes 294944 | tf_op jit(solution)/shard_map/all_to_all | solution.py:131
  311.4 21.3 %collective-permute-done.1 = f32[2,144,128]{2,1,0:T(8,128)S(1)} collective-permute-done((f32[2,144,128]{2,1,0:T(8,128)S(1)}, f32[2,144,128]{2,1,0:T(8,128)S(1)}, u32[]{:S(2)}, u32[]{:S(2)}) %collective-permute-start.1) | collective-permute-done | bytes 147488 | tf_op jit(solution)/shard_map/ppermute | solution.py:134
  335.1 5.4 %collective-permute-done.2 = f32[144,128]{1,0:T(8,128)S(1)} collective-permute-done((f32[144,128]{1,0:T(8,128)S(1)}, f32[144,128]{1,0:T(8,128)S(1)}, u32[]{:S(2)}, u32[]{:S(2)}) %collective-permute-start.2) | collective-permute-done | bytes 73760 | tf_op jit(solution)/shard_map/ppermute | solution.py:138
  (81 shorter events, 44.7 us)
Async XLA Ops:
  7.2 2.0 copy-start.2
  7.2 112.3 %all-gather.2.cloned.1.call-start = ((), (), s32[]{:S(2)}) async-start(), calls=%async_computation.12 | async-start | bytes 4718592 | tf_op jit(solution)/shard_map/all_gather | solution.py:58
  11.5 4.6 %copy-start.3 = (bf16[144,4096]{1,0:T(8,128)(2,1)S(1)}, bf16[144,4096]{1,0:T(8,128)(2,1)}, u32[]{:S(2)}) copy-start(bf16[144,4096]{1,0:T(8,128)(2,1)} %param.18) | copy-start | bytes 3538948
  11.5 21.1 %all-to-all-start.2 = ((bf16[4,144,1024]{2,1,0:T(8,128)(2,1)}), bf16[4,144,1024]{2,1,0:T(8,128)(2,1)S(1)}, u32[]{:S(2)}, u32[]{:S(2)}) async-start(bf16[4,144,1024]{2,1,0:T(8,128)(2,1)} %copy.29), calls=%async_computation.2 | async-start | bytes 2359296 | tf_op jit(solution)/shard_map/all_to_all | solution.py:25
  32.6 90.9 %all-to-all-start = ((bf16[4,144,1024]{2,1,0:T(8,128)(2,1)}), bf16[4,144,1024]{2,1,0:T(8,128)(2,1)S(1)}, u32[]{:S(2)}, u32[]{:S(2)}) async-start(bf16[4,144,1024]{2,1,0:T(8,128)(2,1)} %copy.28), calls=%async_computation | async-start | bytes 2359296 | tf_op jit(solution)/shard_map/all_to_all | solution.py:25
  123.5 21.0 %all-to-all-start.3 = ((bf16[4,144,1024]{2,1,0:T(8,128)(2,1)}), bf16[4,144,1024]{2,1,0:T(8,128)(2,1)S(1)}, u32[]{:S(2)}, u32[]{:S(2)}) async-start(bf16[4,144,1024]{2,1,0:T(8,128)(2,1)} %bitcast.11), calls=%async_computation.3 | async-start | bytes 2359296 | tf_op jit(solution)/shard_map/all_to_all | solution.py:36
  144.5 18.6 %all-to-all-start.1 = ((bf16[4,144,1024]{2,1,0:T(8,128)(2,1)}), bf16[4,144,1024]{2,1,0:T(8,128)(2,1)S(1)}, u32[]{:S(2)}, u32[]{:S(2)}) async-start(bf16[4,144,1024]{2,1,0:T(8,128)(2,1)} %bitcast.5), calls=%async_computation.1 | async-start | bytes 2359296 | tf_op jit(solution)/shard_map/all_to_all | solution.py:36
  148.3 15.1 %copy-start.4 = (bf16[144,1024]{1,0:T(8,128)(2,1)S(1)}, bf16[144,1024]{1,0:T(8,128)(2,1)}, u32[]{:S(2)}) copy-start(bf16[144,1024]{1,0:T(8,128)(2,1)} %param.15) | copy-start | bytes 884740
  148.3 15.1 %copy-start.5 = (bf16[144,1024]{1,0:T(8,128)(2,1)S(1)}, bf16[144,1024]{1,0:T(8,128)(2,1)}, u32[]{:S(2)}) copy-start(bf16[144,1024]{1,0:T(8,128)(2,1)} %param.13) | copy-start | bytes 884740
  148.3 15.1 %copy-start.6 = (bf16[144,1024]{1,0:T(8,128)(2,1)S(1)}, bf16[144,1024]{1,0:T(8,128)(2,1)}, u32[]{:S(2)}) copy-start(bf16[144,1024]{1,0:T(8,128)(2,1)} %param.14) | copy-start | bytes 884740
  148.3 15.1 %copy-start.7 = (f32[144]{0:T(256)S(1)}, f32[144]{0:T(256)}, u32[]{:S(2)}) copy-start(f32[144]{0:T(256)} %param.16) | copy-start | bytes 1732
  148.3 15.1 %copy-start.9 = (f32[144]{0:T(256)S(1)}, f32[144]{0:T(256)}, u32[]{:S(2)}) copy-start(f32[144]{0:T(256)} %param.17) | copy-start | bytes 1732
  163.4 34.8 %copy-start.8 = (s32[16]{0:T(128)S(1)}, s32[16]{0:T(128)}, u32[]{:S(2)}) copy-start(s32[16]{0:T(128)} %param.20) | copy-start | bytes 196
  173.2 21.0 %all-to-all-start.5 = ((f32[8,4,1024]{2,1,0:T(4,128)}), f32[8,4,1024]{2,1,0:T(4,128)S(1)}, u32[]{:S(2)}, u32[]{:S(2)}) async-start(f32[8,4,1024]{2,1,0:T(4,128)} %broadcast_in_dim.13), calls=%async_computation.5 | async-start | bytes 262144 | tf_op jit(solution)/shard_map/all_to_all | solution.py:15
  194.9 8.5 %all-to-all-start.7 = ((f32[4,1,144]{2,1,0:T(1,128)}), f32[4,1,144]{2,1,0:T(1,128)S(1)}, u32[]{:S(2)}, u32[]{:S(2)}) async-start(f32[4,1,144]{2,1,0:T(1,128)} %broadcast_in_dim.15), calls=%async_computation.7 | async-start | bytes 8192 | tf_op jit(solution)/shard_map/all_to_all | solution.py:15
  204.0 19.9 %all-to-all-start.6 = ((f32[16,1,16]{2,1,0:T(1,128)}), f32[16,1,16]{2,1,0:T(1,128)S(1)}, u32[]{:S(2)}, u32[]{:S(2)}) async-start(f32[16,1,16]{2,1,0:T(1,128)} %broadcast_in_dim.14), calls=%async_computation.6 | async-start | bytes 16384 | tf_op jit(solution)/shard_map/all_to_all | solution.py:15
  225.0 3.7 %copy-start.10 = (s32[128,2]{0,1:T(2,128)S(1)}, s32[128,2]{0,1:T(2,128)}, u32[]{:S(2)}) copy-start(s32[128,2]{0,1:T(2,128)} %param.21) | copy-start | bytes 3076
  225.0 20.4 %all-to-all-start.8 = ((bf16[4,144,1024]{2,1,0:T(8,128)(2,1)}), bf16[4,144,1024]{2,1,0:T(8,128)(2,1)S(1)}, u32[]{:S(2)}, u32[]{:S(2)}) async-start(bf16[4,144,1024]{2,1,0:T(8,128)(2,1)} %broadcast_in_dim.16), calls=%async_computation.8 | async-start | bytes 2359296 | tf_op jit(solution)/shard_map/all_to_all | solution.py:15
  235.2 16.0 %copy-start.11 = (f32[128]{0:T(128)}, f32[128]{0:T(128)S(1)}, u32[]{:S(2)}) copy-start(f32[128]{0:T(128)S(1)} %get-tuple-element.8) | copy-start | bytes 1540
  247.6 19.4 %all-to-all-start.9 = ((bf16[4,144,1024]{2,1,0:T(8,128)(2,1)}), bf16[4,144,1024]{2,1,0:T(8,128)(2,1)S(1)}, u32[]{:S(2)}, u32[]{:S(2)}) async-start(bf16[4,144,1024]{2,1,0:T(8,128)(2,1)} %broadcast_in_dim.17), calls=%async_computation.9 | async-start | bytes 2359296 | tf_op jit(solution)/shard_map/all_to_all | solution.py:15
  271.4 4.7 %collective-permute-start = (f32[576,2,256]{2,0,1:T(8,128)S(1)}, f32[576,2,256]{2,0,1:T(8,128)S(1)}, u32[]{:S(2)}, u32[]{:S(2)}) collective-permute-start(f32[576,2,256]{2,0,1:T(8,128)S(1)} %dynamic-slice_bitcast_fusion), channel_id=1, source_target_pairs={{0,32},{32,0},{1,33},{33,1},{2,34},{34,2},{3,35},{35,3},{4,36},{36... | collective-permute-start | bytes 3538952 | tf_op jit(solution)/shard_map/ppermute | solution.py:128
  298.6 10.3 %all-to-all-start.11 = ((f32[4,144,128]{2,1,0:T(8,128)}), f32[4,144,128]{2,1,0:T(8,128)S(1)}, u32[]{:S(2)}, u32[]{:S(2)}) async-start(f32[4,144,128]{2,1,0:T(8,128)} %bitcast.25), calls=%async_computation.11 | async-start | bytes 589824 | tf_op jit(solution)/shard_map/all_to_all | solution.py:131
  308.9 23.8 %collective-permute-start.1 = (f32[2,144,128]{2,1,0:T(8,128)S(1)}, f32[2,144,128]{2,1,0:T(8,128)S(1)}, u32[]{:S(2)}, u32[]{:S(2)}) collective-permute-start(f32[2,144,128]{2,1,0:T(8,128)S(1)} %dynamic-slice_bitcast_fusion.1), channel_id=1, source_target_pairs={{0,256},{256,0},{1,257},{257,1},{2,258},{258,2},{3,259},{259,3},{4... | collective-permute-start | bytes 442376 | tf_op jit(solution)/shard_map/ppermute | solution.py:134
  332.7 7.8 %collective-permute-start.2 = (f32[144,128]{1,0:T(8,128)S(1)}, f32[144,128]{1,0:T(8,128)S(1)}, u32[]{:S(2)}, u32[]{:S(2)}) collective-permute-start(f32[144,128]{1,0:T(8,128)S(1)} %dynamic-slice_bitcast_fusion.2), channel_id=1, source_target_pairs={{0,128},{64,192},{128,0},{192,64},{1,129},{65,193},{129,1},{193,65... | collective-permute-start | bytes 221192 | tf_op jit(solution)/shard_map/ppermute | solution.py:138
  (2 other events, 3.0 us)
Sparse Core Ops, SparseCore 0:
  10.0 109.3 all-gather.1

commit v2 on v1

v2 whole, which is shorter than its diff:
```python
import jax
import jax.numpy as jnp
from jax import lax
from jax.sharding import Mesh, PartitionSpec as P

D = 4608
NX, NY, NZ = 4, 4, 8

beta_scale = 0.1
epsilon = 1e-06


def spread(value, axes, count):
    return lax.all_to_all(jnp.broadcast_to(value[None], (count,) + value.shape), axes, 0, 0)


def swapped(value, axis):
    return lax.ppermute(value, axis, [(0, 1), (1, 0)])


def rows_of_all_y(weight, core):
    rows, features = weight.shape
    half = weight.reshape(rows, NY, 2, NZ // 2, 128)
    half = lax.dynamic_index_in_dim(half, core, 2, keepdims=False)
    half = half.transpose(0, 2, 1, 3).reshape(rows, features // 2)
    mine = spread(half, "y", NY).reshape(NY * rows, features // 2)
    halves = jnp.broadcast_to(mine[None], (2,) + mine.shape)
    return lax.dynamic_update_index_in_dim(halves, swapped(mine, "c"), 1 - core, 0)


def hidden_of(weight, context, stream):
    depth = weight.shape[2]
    for half in range(2):
        stream = stream.astype(jnp.float32) + lax.dot_general(
            weight[half],
            context[:, half * depth : (half + 1) * depth],
            (((1,), (1,)), ((), ())),
            preferred_element_type=jnp.float32,
        )
    return stream


def shards(
    policy_context,
    frozen_context,
    policy_stream,
    frozen_stream,
    targets,
    policy_gain,
    frozen_gain,
    policy_weight,
    frozen_weight,
    valid_lengths,
    pair_rows,
):
    rows, tokens_here = policy_stream.shape
    seq_len = tokens_here // valid_lengths.shape[0]
    seqs = valid_lengths.shape[0] // NY
    tokens = tokens_here // NY
    z_hi, core, y = lax.axis_index("zh"), lax.axis_index("c"), lax.axis_index("y")

    contexts = jnp.stack(
        [policy_context.reshape(NY, tokens, 128), frozen_context.reshape(NY, tokens, 128)], axis=1
    )
    contexts = lax.all_to_all(contexts, "y", 0, 0)
    contexts = contexts.transpose(1, 2, 0, 3).reshape(2 * tokens, NY * 128)
    contexts = lax.all_gather(contexts, "zl", axis=1, tiled=True)

    frozen_rows = rows_of_all_y(frozen_weight, core)
    policy_rows = rows_of_all_y(policy_weight, core)
    streams = jnp.stack(
        [
            s.reshape(rows, NY, tokens).transpose(1, 0, 2)
            for s in (policy_stream, frozen_stream, targets)
        ],
        axis=1,
    )
    streams = lax.all_to_all(streams, "y", 0, 0)
    streams = [streams[:, i].reshape(NY * rows, tokens) for i in range(3)]
    gains = spread(jnp.stack([policy_gain, frozen_gain]), "y", NY)
    gains = [gains[:, i].reshape(NY * rows, 1) for i in range(2)]
    contexts, frozen_rows, policy_rows, streams, gains = lax.optimization_barrier(
        (contexts, frozen_rows, policy_rows, streams, gains)
    )

    policy_columns, frozen_columns = contexts[:tokens], contexts[tokens:]
    frozen_hidden = hidden_of(frozen_rows, frozen_columns, streams[1])
    policy_hidden = hidden_of(policy_rows, policy_columns, streams[0])
    target_values = streams[2].astype(jnp.float32)
    policy_weighted = gains[0] * target_values
    frozen_weighted = gains[1] * target_values
    stats = jnp.stack(
        [
            jnp.sum(policy_hidden * policy_hidden, axis=0),
            jnp.sum(policy_hidden * policy_weighted, axis=0),
            jnp.sum(frozen_hidden * frozen_hidden, axis=0),
            jnp.sum(frozen_hidden * frozen_weighted, axis=0),
        ]
    )
    stats = jnp.sum(spread(stats, "zl", NZ), axis=0)

    policy_scale = lax.rsqrt(stats[0] / D + epsilon)
    frozen_scale = lax.rsqrt(stats[2] / D + epsilon)
    policy_dotted = stats[1]
    gap_of_token = policy_scale * policy_dotted - frozen_scale * stats[3]
    lengths = lax.dynamic_slice_in_dim(valid_lengths, y * seqs, seqs, 0)
    positions = lax.broadcasted_iota(jnp.int32, (seqs, seq_len), 1)
    valid = (positions < lengths[:, None]).astype(jnp.float32)
    own_gaps = jnp.sum(gap_of_token.reshape(seqs, seq_len) * valid, axis=1)
    other_gaps = swapped(own_gaps, "c")
    chip_gaps = jnp.where(
        core == 0, jnp.stack([own_gaps, other_gaps]), jnp.stack([other_gaps, own_gaps])
    )
    gaps = spread(chip_gaps, ("zh", "x", "y"), 2 * NX * NY)
    gaps = gaps.reshape(2 * NX, NY, 2, seqs).transpose(0, 2, 1, 3).reshape(-1)

    total_seqs = gaps.shape[0]
    pair_count = pair_rows.shape[0]
    row_ids = lax.broadcasted_iota(jnp.int32, (pair_count, total_seqs), 1)
    signs = (row_ids == pair_rows[:, 0:1]).astype(jnp.float32) - (
        row_ids == pair_rows[:, 1:2]
    ).astype(jnp.float32)
    margins = beta_scale * jnp.sum(signs * gaps[None, :], axis=1)
    loss = jnp.sum(jax.nn.softplus(-margins))
    slopes = -jax.nn.sigmoid(-margins)
    own_ids = (
        (lax.axis_index(("zh", "x", "c")) * NY + y) * seqs
        + lax.broadcasted_iota(jnp.int32, (1, seqs), 1)
    )
    own_chosen = (pair_rows[:, 0:1] == own_ids).astype(jnp.float32)
    own_rejected = (pair_rows[:, 1:2] == own_ids).astype(jnp.float32)
    coef = beta_scale * jnp.sum(slopes[:, None] * (own_chosen - own_rejected), axis=0)
    token_coef = (coef[:, None] * valid).reshape(tokens)
    step_size = token_coef * policy_scale
    correction = policy_dotted * policy_scale * policy_scale / D
    hidden_grad = (
        step_size[None, :] * (policy_weighted - policy_hidden * correction[None, :])
    ).astype(jnp.bfloat16)

    columns = policy_columns.reshape(tokens, 2, 2, 2, 2, 2, 128).transpose(2, 4, 0, 5, 1, 3, 6)
    columns = columns.reshape(4, tokens, NX, 256)

    def grad_of(core, z_hi):
        piece = lax.dynamic_index_in_dim(columns, 2 * core + z_hi, 0, keepdims=False)
        return lax.dot_general(
            hidden_grad, piece, (((1,), (0,)), ((), ())), preferred_element_type=jnp.float32
        ).transpose(1, 0, 2)

    z_order = (1 - z_hi, z_hi)
    arrived = [swapped(grad_of(1 - core, z).astype(jnp.bfloat16), "c") for z in z_order]
    sums = []
    for z, piece in zip(z_order, arrived):
        grad = (grad_of(core, z) + piece.astype(jnp.float32)).astype(jnp.bfloat16)
        grad = lax.all_to_all(grad.reshape(NX * NY, rows, 256), ("x", "y"), 0, 0)
        sums.append(jnp.sum(grad.astype(jnp.float32), axis=0))
    weight_grad = sums[1] + swapped(sums[0], "zh")
    return (weight_grad, margins, loss)


def solution(mesh):
    dp, blk = ("zh", "x", "c"), ("y", "zl")
    fine = Mesh(mesh.devices.reshape(2, NX, 2, NY, NZ), dp + blk)
    placed = (
        P(dp, blk),
        P(dp, blk),
        P(blk, dp),
        P(blk, dp),
        P(blk, dp),
        P(blk),
        P(blk),
        P(blk, None),
        P(blk, None),
        P(dp),
        P(),
    )
    return jax.shard_map(
        shards, mesh=fine, in_specs=placed, out_specs=(P(blk, dp), P(), P()), check_vma=False
    )
```

time: 349 us -> 276 us (0.79)
  the two profiles are of different devices: /device:TPU:32 before, /device:TPU:35 now
where the time goes in v2:
time: 276 us; the launch traced here: 275 us
  waiting for transfers between devices  118 us (43%)
  starting transfers between devices  73.2 us (27%)
  local copies, waits for them, and re-layouts  32.4 us (12%)
  matrix products  18 us (7%)
  between operations  14.5 us (5%)
  blocking collectives  12.6 us (5%)
  other arithmetic  5.77 us (2%)
    all_to_all x5, waiting for transfers between devices, spread(): lax.all_to_all(jnp.broadcast_to(value[None], (count,) + value.shape), axe...  69.3 us
    all_to_all x5, starting transfers between devices, spread(): lax.all_to_all(jnp.broadcast_to(value[None], (count,) + value.shape), axe...  35.3 us
    all_to_all x2, waiting for transfers between devices, shards(): grad = lax.all_to_all(grad.reshape(NX * NY, rows, 256), ('x', 'y'), 0, 0)  24 us
    ppermute x6, starting transfers between devices, swapped(): return lax.ppermute(value, axis, [(0, 1), (1, 0)])  22.9 us
    ppermute x6, waiting for transfers between devices, swapped(): return lax.ppermute(value, axis, [(0, 1), (1, 0)])  13.2 us
    all_to_all x1, blocking collectives, shards(): contexts = lax.all_to_all(contexts, 'y', 0, 0)  12.6 us
    all_to_all x1, waiting for transfers between devices, shards(): streams = lax.all_to_all(streams, 'y', 0, 0)  11.9 us
    all_to_all x2, starting transfers between devices, shards(): grad = lax.all_to_all(grad.reshape(NX * NY, rows, 256), ('x', 'y'), 0, 0)  11.4 us
  transfers between devices with their start and end apart: 15, of which 10 were waited for; matrix products, arithmetic and copies ran while one was open for 13% of the time, Pallas kernels for 0%

profile of v2, /device:TPU:35, one launch (start us, length us, event | category | flops | bytes accessed | tf_op | source)
XLA Modules:
  0.0 274.7 jit_solution(3742923225125618659)
XLA Ops:
  8.4 12.6 %all_to_all.45 = bf16[4,2,256,128]{3,2,1,0:T(8,128)(2,1)S(1)} all-to-all(bf16[4,2,256,128]{3,2,1,0:T(8,128)(2,1)S(1)} %pad_maximum_fusion.1), channel_id=1, replica_groups=mesh['zh'=2,'x'=4,'c'=2,'y'=4,'zl'=8] {'y'}, dimensions={0} | all-to-all | bytes 1048576 | tf_op jit(solution)/shard_map/all_to_all | solution.py:65
  26.9 3.6 %all-to-all-start.2 = ((bf16[4,144,2048]{2,1,0:T(8,128)(2,1)}), bf16[4,144,2048]{2,1,0:T(8,128)(2,1)S(1)}, u32[]{:S(2)}, u32[]{:S(2)}) async-start(bf16[4,144,2048]{2,1,0:T(8,128)(2,1)} %broadcast_in_dim.64), calls=%async_computation.2 | async-start | bytes 4718592 | tf_op jit(solution)/shard_map/all_to_all | solution.py:14
  31.2 26.6 %all-to-all-done.2 = bf16[4,144,2048]{2,1,0:T(8,128)(2,1)S(1)} async-done(((bf16[4,144,2048]{2,1,0:T(8,128)(2,1)}), bf16[4,144,2048]{2,1,0:T(8,128)(2,1)S(1)}, u32[]{:S(2)}, u32[]{:S(2)}) %all-to-all-start.2) | async-done | bytes 2359328 | tf_op jit(solution)/shard_map/all_to_all | solution.py:14
  59.5 4.6 %all-to-all-start.1 = ((bf16[4,144,2048]{2,1,0:T(8,128)(2,1)}), bf16[4,144,2048]{2,1,0:T(8,128)(2,1)}, u32[]{:S(2)}, u32[]{:S(2)}) async-start(bf16[4,144,2048]{2,1,0:T(8,128)(2,1)} %broadcast_in_dim.30), calls=%async_computation.1 | async-start | bytes 4718592 | tf_op jit(solution)/shard_map/all_to_all | solution.py:14
  64.2 4.7 %collective-permute-start.1 = (bf16[576,2048]{1,0:T(8,128)(2,1)S(1)}, bf16[576,2048]{1,0:T(8,128)(2,1)}, u32[]{:S(2)}, u32[]{:S(2)}) collective-permute-start(bf16[576,2048]{1,0:T(8,128)(2,1)S(1)} %bitcast.110), channel_id=1, source_target_pairs={{0,32},{32,0},{1,33},{33,1},{2,34},{34,2},{3,35},{35,3},{4,36},{36... | collective-permute-start | bytes 7077896 | tf_op jit(solution)/shard_map/ppermute | solution.py:18
  68.9 21.8 %all-to-all-done.1 = bf16[4,144,2048]{2,1,0:T(8,128)(2,1)} async-done(((bf16[4,144,2048]{2,1,0:T(8,128)(2,1)}), bf16[4,144,2048]{2,1,0:T(8,128)(2,1)}, u32[]{:S(2)}, u32[]{:S(2)}) %all-to-all-start.1) | async-done | bytes 2359328 | tf_op jit(solution)/shard_map/all_to_all | solution.py:14
  90.7 5.6 %collective-permute-start = (bf16[576,2048]{1,0:T(8,128)(2,1)}, bf16[576,2048]{1,0:T(8,128)(2,1)}, u32[]{:S(2)}, u32[]{:S(2)}) collective-permute-start(bf16[576,2048]{1,0:T(8,128)(2,1)} %bitcast.7), channel_id=1, source_target_pairs={{0,32},{32,0},{1,33},{33,1},{2,34},{34,2},{3,35},{35,3},{4,36},{36... | collective-permute-start | bytes 7077896 | tf_op jit(solution)/shard_map/ppermute | solution.py:18
  96.9 3.2 %all-to-all-start.4 = ((f32[4,2,144]{2,1,0:T(2,128)}), f32[4,2,144]{2,1,0:T(2,128)S(1)}, u32[]{:S(2)}, u32[]{:S(2)}) async-start(f32[4,2,144]{2,1,0:T(2,128)} %broadcast_in_dim.68), calls=%async_computation.4 | async-start | bytes 16384 | tf_op jit(solution)/shard_map/all_to_all | solution.py:14
  104.3 3.5 %all-to-all-start.3 = ((bf16[4,3,144,256]{3,2,1,0:T(8,128)(2,1)}), bf16[4,3,144,256]{3,2,1,0:T(8,128)(2,1)S(1)}, u32[]{:S(2)}, u32[]{:S(2)}) async-start(bf16[4,3,144,256]{3,2,1,0:T(8,128)(2,1)} %copy.77), calls=%async_computation.3 | async-start | bytes 1769472 | tf_op jit(solution)/shard_map/all_to_all | solution.py:78
  108.1 11.9 %all-to-all-done.3 = bf16[4,3,144,256]{3,2,1,0:T(8,128)(2,1)S(1)} async-done(((bf16[4,3,144,256]{3,2,1,0:T(8,128)(2,1)}), bf16[4,3,144,256]{3,2,1,0:T(8,128)(2,1)S(1)}, u32[]{:S(2)}, u32[]{:S(2)}) %all-to-all-start.3) | async-done | bytes 884768 | tf_op jit(solution)/shard_map/all_to_all | solution.py:78
  123.7 6.2 %broadcast_in_dim.61 = bf16[2,576,2048]{2,1,0:T(8,128)(2,1)} broadcast(bf16[576,2048]{1,0:T(8,128)(2,1)} %bitcast.7), dimensions={1,2} | broadcast | bytes 7077888 | tf_op jit(solution)/shard_map/broadcast_in_dim | solution.py:27
  129.9 3.4 %bitcast_dynamic-update-slice_fusion.1 = bf16[2,576,2048]{2,1,0:T(8,128)(2,1)} fusion(bf16[2,576,2048]{2,1,0:T(8,128)(2,1)} %broadcast_in_dim.61, s32[]{:T(128)S(6)} %select_n.45, bf16[576,2048]{1,0:T(8,128)(2,1)} %collective-permute-done), kind=kLoop, calls=%fused_computation.13 | loop fusion | bytes 4718596 | tf_op jit(solution)/shard_map/jit(dynamic_update_index_in_dim)/dynamic_update_slice | solution.py:28
  138.9 2.9 %fusion.16 = f32[576,256]{1,0:T(8,128)S(1)} fusion(bf16[2,576,2048]{2,1,0:T(8,128)(2,1)} %copy-done.2, bf16[512,4096]{1,0:T(8,128)(2,1)} %all-gather.2.cloned.1.call-done, f32[576,256]{1,0:T(8,128)S(1)} %fusion.8, bf16[576,256]{1,0:T(8,128)(2,1)S(1)} %bitcast.130), kind=kOutput, calls=%fused_computation.24 | convolution fusion | flops 604422144 | bytes 4882432 | tf_op jit(solution)/shard_map/dot_general | solution.py:34
  145.4 12.9 %all-to-all-start.5 = ((f32[8,4,256]{2,1,0:T(4,128)}), f32[8,4,256]{2,1,0:T(4,128)S(1)}, u32[]{:S(2)}, u32[]{:S(2)}) async-start(f32[8,4,256]{2,1,0:T(4,128)} %broadcast_in_dim.69), calls=%async_computation.5 | async-start | bytes 65536 | tf_op jit(solution)/shard_map/all_to_all | solution.py:14
  158.3 8.2 %all-to-all-done.5 = f32[8,4,256]{2,1,0:T(4,128)S(1)} async-done(((f32[8,4,256]{2,1,0:T(4,128)}), f32[8,4,256]{2,1,0:T(4,128)S(1)}, u32[]{:S(2)}, u32[]{:S(2)}) %all-to-all-start.5) | async-done | bytes 32800 | tf_op jit(solution)/shard_map/all_to_all | solution.py:14
  166.8 5.0 %collective-permute-start.2 = (f32[4]{0:T(128)S(1)}, f32[4]{0:T(128)S(1)}, u32[]{:S(2)}, u32[]{:S(2)}) collective-permute-start(f32[4]{0:T(128)S(1)} %select_reduce_fusion), channel_id=1, source_target_pairs={{0,32},{32,0},{1,33},{33,1},{2,34},{34,2},{3,35},{35,3},{4,36},{36... | collective-permute-start | bytes 56 | tf_op jit(solution)/shard_map/ppermute | solution.py:18
  173.3 10.9 %all-to-all-start.6 = ((f32[32,2,4]{2,1,0:T(2,128)}), f32[32,2,4]{2,1,0:T(2,128)S(1)}, u32[]{:S(2)}, u32[]{:S(2)}) async-start(f32[32,2,4]{2,1,0:T(2,128)} %broadcast_in_dim.70), calls=%async_computation.6 | async-start | bytes 65536 | tf_op jit(solution)/shard_map/all_to_all | solution.py:14
  188.4 11.1 %all-to-all-done.6 = f32[32,2,4]{2,1,0:T(2,128)S(1)} async-done(((f32[32,2,4]{2,1,0:T(2,128)}), f32[32,2,4]{2,1,0:T(2,128)S(1)}, u32[]{:S(2)}, u32[]{:S(2)}) %all-to-all-start.6) | async-done | bytes 1056 | tf_op jit(solution)/shard_map/all_to_all | solution.py:14
  202.9 3.4 %collective-permute-start.4 = (bf16[4,576,256]{2,1,0:T(8,128)(2,1)}, bf16[4,576,256]{2,1,0:T(8,128)(2,1)}, u32[]{:S(2)}, u32[]{:S(2)}) collective-permute-start(bf16[4,576,256]{2,1,0:T(8,128)(2,1)} %fusion.15), channel_id=1, source_target_pairs={{0,32},{32,0},{1,33},{33,1},{2,34},{34,2},{3,35},{35,3},{4,36},{36... | collective-permute-start | bytes 3538952 | tf_op jit(solution)/shard_map/ppermute | solution.py:18
  212.7 5.3 %all-to-all-start.8 = ((bf16[16,144,256]{2,1,0:T(8,128)(2,1)}), bf16[16,144,256]{2,1,0:T(8,128)(2,1)}, u32[]{:S(2)}, u32[]{:S(2)}) async-start(bf16[16,144,256]{2,1,0:T(8,128)(2,1)} %bitcast.117), calls=%async_computation.8 | async-start | bytes 2359296 | tf_op jit(solution)/shard_map/all_to_all | solution.py:154
  220.9 13.1 %all-to-all-done.8 = bf16[16,144,256]{2,1,0:T(8,128)(2,1)} async-done(((bf16[16,144,256]{2,1,0:T(8,128)(2,1)}), bf16[16,144,256]{2,1,0:T(8,128)(2,1)}, u32[]{:S(2)}, u32[]{:S(2)}) %all-to-all-start.8) | async-done | bytes 1179680 | tf_op jit(solution)/shard_map/all_to_all | solution.py:154
  234.0 6.1 %all-to-all-start.7 = ((bf16[16,144,256]{2,1,0:T(8,128)(2,1)}), bf16[16,144,256]{2,1,0:T(8,128)(2,1)S(1)}, u32[]{:S(2)}, u32[]{:S(2)}) async-start(bf16[16,144,256]{2,1,0:T(8,128)(2,1)} %bitcast.118), calls=%async_computation.7 | async-start | bytes 2359296 | tf_op jit(solution)/shard_map/all_to_all | solution.py:154
  243.8 10.9 %all-to-all-done.7 = bf16[16,144,256]{2,1,0:T(8,128)(2,1)S(1)} async-done(((bf16[16,144,256]{2,1,0:T(8,128)(2,1)}), bf16[16,144,256]{2,1,0:T(8,128)(2,1)S(1)}, u32[]{:S(2)}, u32[]{:S(2)}) %all-to-all-start.7) | async-done | bytes 1179680 | tf_op jit(solution)/shard_map/all_to_all | solution.py:154
  254.8 12.4 %collective-permute-done.5 = f32[144,256]{1,0:T(8,128)S(1)} collective-permute-done((f32[144,256]{1,0:T(8,128)S(1)}, f32[144,256]{1,0:T(8,128)S(1)}, u32[]{:S(2)}, u32[]{:S(2)}) %collective-permute-start.5) | collective-permute-done | bytes 147488 | tf_op jit(solution)/shard_map/ppermute | solution.py:18
  (107 shorter events, 50.4 us)
Async XLA Ops:
  7.2 126.1 %all-gather.2.cloned.1.call-start = ((), (), s32[]{:S(2)}) async-start(), calls=%async_computation.9 | async-start | bytes 4718592 | tf_op jit(solution)/shard_map/all_gather | solution.py:67
  7.2 15.1 %copy-start.4 = (bf16[144,4096]{1,0:T(8,128)(2,1)S(1)}, bf16[144,4096]{1,0:T(8,128)(2,1)}, u32[]{:S(2)}) copy-start(bf16[144,4096]{1,0:T(8,128)(2,1)} %param.19) | copy-start | bytes 3538948
  26.9 30.9 %all-to-all-start.2 = ((bf16[4,144,2048]{2,1,0:T(8,128)(2,1)}), bf16[4,144,2048]{2,1,0:T(8,128)(2,1)S(1)}, u32[]{:S(2)}, u32[]{:S(2)}) async-start(bf16[4,144,2048]{2,1,0:T(8,128)(2,1)} %broadcast_in_dim.64), calls=%async_computation.2 | async-start | bytes 4718592 | tf_op jit(solution)/shard_map/all_to_all | solution.py:14
  59.5 36.7 %copy-start.12 = (f32[144]{0:T(256)S(1)}, f32[144]{0:T(256)}, u32[]{:S(2)}) copy-start(f32[144]{0:T(256)} %param.17) | copy-start | bytes 1732
  59.5 36.7 %copy-start.13 = (f32[144]{0:T(256)S(1)}, f32[144]{0:T(256)}, u32[]{:S(2)}) copy-start(f32[144]{0:T(256)} %param.16) | copy-start | bytes 1732
  59.5 40.6 %copy-start.8 = (bf16[144,1024]{1,0:T(8,128)(2,1)S(1)}, bf16[144,1024]{1,0:T(8,128)(2,1)}, u32[]{:S(2)}) copy-start(bf16[144,1024]{1,0:T(8,128)(2,1)} %param.13) | copy-start | bytes 884740
  59.5 40.8 %copy-start.9 = (bf16[144,1024]{1,0:T(8,128)(2,1)S(1)}, bf16[144,1024]{1,0:T(8,128)(2,1)}, u32[]{:S(2)}) copy-start(bf16[144,1024]{1,0:T(8,128)(2,1)} %param.14) | copy-start | bytes 884740
  59.5 41.1 %copy-start.10 = (bf16[144,1024]{1,0:T(8,128)(2,1)S(1)}, bf16[144,1024]{1,0:T(8,128)(2,1)}, u32[]{:S(2)}) copy-start(bf16[144,1024]{1,0:T(8,128)(2,1)} %param.15) | copy-start | bytes 884740
  59.5 31.1 %all-to-all-start.1 = ((bf16[4,144,2048]{2,1,0:T(8,128)(2,1)}), bf16[4,144,2048]{2,1,0:T(8,128)(2,1)}, u32[]{:S(2)}, u32[]{:S(2)}) async-start(bf16[4,144,2048]{2,1,0:T(8,128)(2,1)} %broadcast_in_dim.30), calls=%async_computation.1 | async-start | bytes 4718592 | tf_op jit(solution)/shard_map/all_to_all | solution.py:14
  64.2 56.7 %collective-permute-start.1 = (bf16[576,2048]{1,0:T(8,128)(2,1)S(1)}, bf16[576,2048]{1,0:T(8,128)(2,1)}, u32[]{:S(2)}, u32[]{:S(2)}) collective-permute-start(bf16[576,2048]{1,0:T(8,128)(2,1)S(1)} %bitcast.110), channel_id=1, source_target_pairs={{0,32},{32,0},{1,33},{33,1},{2,34},{34,2},{3,35},{35,3},{4,36},{36... | collective-permute-start | bytes 7077896 | tf_op jit(solution)/shard_map/ppermute | solution.py:18
  90.7 33.0 %collective-permute-start = (bf16[576,2048]{1,0:T(8,128)(2,1)}, bf16[576,2048]{1,0:T(8,128)(2,1)}, u32[]{:S(2)}, u32[]{:S(2)}) collective-permute-start(bf16[576,2048]{1,0:T(8,128)(2,1)} %bitcast.7), channel_id=1, source_target_pairs={{0,32},{32,0},{1,33},{33,1},{2,34},{34,2},{3,35},{35,3},{4,36},{36... | collective-permute-start | bytes 7077896 | tf_op jit(solution)/shard_map/ppermute | solution.py:18
  96.9 7.4 %all-to-all-start.4 = ((f32[4,2,144]{2,1,0:T(2,128)}), f32[4,2,144]{2,1,0:T(2,128)S(1)}, u32[]{:S(2)}, u32[]{:S(2)}) async-start(f32[4,2,144]{2,1,0:T(2,128)} %broadcast_in_dim.68), calls=%async_computation.4 | async-start | bytes 16384 | tf_op jit(solution)/shard_map/all_to_all | solution.py:14
  104.3 15.7 %all-to-all-start.3 = ((bf16[4,3,144,256]{3,2,1,0:T(8,128)(2,1)}), bf16[4,3,144,256]{3,2,1,0:T(8,128)(2,1)S(1)}, u32[]{:S(2)}, u32[]{:S(2)}) async-start(bf16[4,3,144,256]{3,2,1,0:T(8,128)(2,1)} %copy.77), calls=%async_computation.3 | async-start | bytes 1769472 | tf_op jit(solution)/shard_map/all_to_all | solution.py:78
  142.1 16.2 %copy-start.11 = (s32[128,2]{0,1:T(2,128)S(1)}, s32[128,2]{0,1:T(2,128)}, u32[]{:S(2)}) copy-start(s32[128,2]{0,1:T(2,128)} %param.21) | copy-start | bytes 3076
  144.7 39.5 %slice-start = ((bf16[512,4096]{1,0:T(8,128)(2,1)}), bf16[256,4096]{1,0:T(8,128)(2,1)S(1)}, s32[]{:S(2)}) async-start(bf16[512,4096]{1,0:T(8,128)(2,1)} %all-gather.2.cloned.1.call-done), calls=%async_computation.10 | async-start | bytes 4194304 | tf_op jit(solution)/shard_map/slice | solution.py:86
  145.4 21.1 %all-to-all-start.5 = ((f32[8,4,256]{2,1,0:T(4,128)}), f32[8,4,256]{2,1,0:T(4,128)S(1)}, u32[]{:S(2)}, u32[]{:S(2)}) async-start(f32[8,4,256]{2,1,0:T(4,128)} %broadcast_in_dim.69), calls=%async_computation.5 | async-start | bytes 65536 | tf_op jit(solution)/shard_map/all_to_all | solution.py:14
  166.8 5.8 %collective-permute-start.2 = (f32[4]{0:T(128)S(1)}, f32[4]{0:T(128)S(1)}, u32[]{:S(2)}, u32[]{:S(2)}) collective-permute-start(f32[4]{0:T(128)S(1)} %select_reduce_fusion), channel_id=1, source_target_pairs={{0,32},{32,0},{1,33},{33,1},{2,34},{34,2},{3,35},{35,3},{4,36},{36... | collective-permute-start | bytes 56 | tf_op jit(solution)/shard_map/ppermute | solution.py:18
  173.3 26.2 %all-to-all-start.6 = ((f32[32,2,4]{2,1,0:T(2,128)}), f32[32,2,4]{2,1,0:T(2,128)S(1)}, u32[]{:S(2)}, u32[]{:S(2)}) async-start(f32[32,2,4]{2,1,0:T(2,128)} %broadcast_in_dim.70), calls=%async_computation.6 | async-start | bytes 65536 | tf_op jit(solution)/shard_map/all_to_all | solution.py:14
  200.8 7.1 %copy-start.15 = (f32[128]{0:T(128)}, f32[128]{0:T(128)S(1)}, u32[]{:S(2)}) copy-start(f32[128]{0:T(128)S(1)} %get-tuple-element.26) | copy-start | bytes 1540
  202.9 6.9 %collective-permute-start.4 = (bf16[4,576,256]{2,1,0:T(8,128)(2,1)}, bf16[4,576,256]{2,1,0:T(8,128)(2,1)}, u32[]{:S(2)}, u32[]{:S(2)}) collective-permute-start(bf16[4,576,256]{2,1,0:T(8,128)(2,1)} %fusion.15), channel_id=1, source_target_pairs={{0,32},{32,0},{1,33},{33,1},{2,34},{34,2},{3,35},{35,3},{4,36},{36... | collective-permute-start | bytes 3538952 | tf_op jit(solution)/shard_map/ppermute | solution.py:18
  207.9 10.1 %collective-permute-start.3 = (bf16[4,576,256]{2,1,0:T(8,128)(2,1)}, bf16[4,576,256]{2,1,0:T(8,128)(2,1)}, u32[]{:S(2)}, u32[]{:S(2)}) collective-permute-start(bf16[4,576,256]{2,1,0:T(8,128)(2,1)} %fusion.14), channel_id=1, source_target_pairs={{0,32},{32,0},{1,33},{33,1},{2,34},{34,2},{3,35},{35,3},{4,36},{36... | collective-permute-start | bytes 3538952 | tf_op jit(solution)/shard_map/ppermute | solution.py:18
  212.7 21.3 %all-to-all-start.8 = ((bf16[16,144,256]{2,1,0:T(8,128)(2,1)}), bf16[16,144,256]{2,1,0:T(8,128)(2,1)}, u32[]{:S(2)}, u32[]{:S(2)}) async-start(bf16[16,144,256]{2,1,0:T(8,128)(2,1)} %bitcast.117), calls=%async_computation.8 | async-start | bytes 2359296 | tf_op jit(solution)/shard_map/all_to_all | solution.py:154
  234.0 20.6 %all-to-all-start.7 = ((bf16[16,144,256]{2,1,0:T(8,128)(2,1)}), bf16[16,144,256]{2,1,0:T(8,128)(2,1)S(1)}, u32[]{:S(2)}, u32[]{:S(2)}) async-start(bf16[16,144,256]{2,1,0:T(8,128)(2,1)} %bitcast.118), calls=%async_computation.7 | async-start | bytes 2359296 | tf_op jit(solution)/shard_map/all_to_all | solution.py:154
  241.5 25.6 %collective-permute-start.5 = (f32[144,256]{1,0:T(8,128)S(1)}, f32[144,256]{1,0:T(8,128)S(1)}, u32[]{:S(2)}, u32[]{:S(2)}) collective-permute-start(f32[144,256]{1,0:T(8,128)S(1)} %convert_reduce_fusion), channel_id=1, source_target_pairs={{0,256},{256,0},{1,257},{257,1},{2,258},{258,2},{3,259},{259,3},{4... | collective-permute-start | bytes 442376 | tf_op jit(solution)/shard_map/ppermute | solution.py:18
  (8 other events, 30.7 us)
Sparse Core Ops, SparseCore 0:
  22.4 98.5 all-gather.1

commit v3 on v2

v3 whole, which is shorter than its diff:
```python
import jax
import jax.numpy as jnp
from jax import lax
from jax.experimental import pallas as pl
from jax.experimental.pallas import tpu as pltpu
from jax.sharding import Mesh, PartitionSpec as P

D = 4608
NX, NY, NZ = 4, 4, 8

beta_scale = 0.1
epsilon = 1e-06


def spread(value, axes, count):
    return lax.all_to_all(jnp.broadcast_to(value[None], (count,) + value.shape), axes, 0, 0)


def swapped(value, axis):
    return lax.ppermute(value, axis, [(0, 1), (1, 0)])


def rows_of_all_y(weight, core):
    rows, features = weight.shape
    half = lax.dynamic_slice_in_dim(weight, core * (rows // 2), rows // 2, 0)
    half = half.reshape(rows // 2, NY, NZ, 128).transpose(0, 2, 1, 3).reshape(rows // 2, features)
    mine = spread(half, "y", NY).reshape(NY * rows // 2, features)
    return mine, swapped(mine, "c")


def own_first(value, core):
    return [
        lax.dynamic_index_in_dim(value, i, 1, keepdims=False).reshape(-1, value.shape[-1])
        for i in (core, 1 - core)
    ]


def forward_step(
    core_ref,
    context_ref,
    policy_mine_ref,
    policy_other_ref,
    frozen_mine_ref,
    frozen_other_ref,
    policy_stream_ref,
    frozen_stream_ref,
    targets_ref,
    gains_ref,
    hidden_ref,
    stats_ref,
    own_columns_ref,
    other_columns_ref,
    frozen_ref,
):
    step = pl.program_id(0)
    tokens = hidden_ref.shape[2]

    @pl.when(step == 0)
    def _():
        hidden_ref[...] = policy_stream_ref[...].astype(jnp.float32)
        frozen_ref[...] = frozen_stream_ref[...].astype(jnp.float32)

    policy_context = context_ref[:tokens, :]
    frozen_context = context_ref[tokens:, :]
    for sums, half, weight, context in (
        (hidden_ref, 0, policy_mine_ref, policy_context),
        (hidden_ref, 1, policy_other_ref, policy_context),
        (frozen_ref, 0, frozen_mine_ref, frozen_context),
        (frozen_ref, 1, frozen_other_ref, frozen_context),
    ):
        sums[half] += lax.dot_general(
            weight[...], context, (((1,), (1,)), ((), ())), preferred_element_type=jnp.float32
        )

    def move(columns_ref):
        for i in range(2 * NY):
            e, y = i // NY, i % NY
            columns_ref[y // 2, 2 * (y % 2) + lax.div(step, 2), :, e * 128 : (e + 1) * 128] = (
                context_ref[:tokens, i * 128 : (i + 1) * 128]
            )

    @pl.when(lax.rem(step, 2) == core_ref[0])
    def _():
        move(own_columns_ref)

    @pl.when(lax.rem(step, 2) != core_ref[0])
    def _():
        move(other_columns_ref)

    @pl.when(step == NZ // 2 - 1)
    def _():
        totals = [0.0] * 4
        for half in range(2):
            target = targets_ref[half].astype(jnp.float32)
            for model, hidden in enumerate((hidden_ref[half], frozen_ref[half])):
                gain = gains_ref[:, 2 * model + half : 2 * model + half + 1]
                terms = (hidden * hidden, hidden * (gain * target))
                for i, term in enumerate(terms):
                    totals[2 * model + i] += jnp.sum(term, axis=0, keepdims=True)
        for i in range(4):
            stats_ref[:, i : i + 1, :] = jnp.broadcast_to(totals[i][None], (NZ, 1, tokens))


def forward(core, contexts, policy_rows, frozen_rows, streams, gains):
    half_rows, features = policy_rows[0].shape
    tokens = contexts.shape[0] // 2
    depth = features // (NZ // 2)

    def whole(*shape):
        return pl.BlockSpec(shape, lambda z: (0,) * len(shape))

    weight = pl.BlockSpec((half_rows, depth), lambda z: (0, z))
    block = (2, half_rows, tokens)
    columns = (2, NX, tokens, 256)
    return pl.pallas_call(
        forward_step,
        grid=(NZ // 2,),
        in_specs=[
            pl.BlockSpec(memory_space=pltpu.SMEM),
            pl.BlockSpec((2 * tokens, depth), lambda z: (0, z)),
            weight,
            weight,
            weight,
            weight,
            whole(*block),
            whole(*block),
            whole(*block),
            whole(half_rows, 4),
        ],
        out_specs=[whole(*block), whole(NZ, 4, tokens), whole(*columns), whole(*columns)],
        out_shape=[
            jax.ShapeDtypeStruct(block, jnp.float32),
            jax.ShapeDtypeStruct((NZ, 4, tokens), jnp.float32),
            jax.ShapeDtypeStruct(columns, jnp.bfloat16),
            jax.ShapeDtypeStruct(columns, jnp.bfloat16),
        ],
        scratch_shapes=[pltpu.VMEM(block, jnp.float32)],
        compiler_params=pltpu.CompilerParams(vmem_limit_bytes=56 * 2**20),
        cost_estimate=pl.CostEstimate(
            flops=8 * half_rows * tokens * features,
            bytes_accessed=2 * features * (4 * half_rows + 3 * tokens),
            transcendentals=0,
        ),
    )(core[None], contexts, *policy_rows, *frozen_rows, *streams, gains)


def shards(
    policy_context,
    frozen_context,
    policy_stream,
    frozen_stream,
    targets,
    policy_gain,
    frozen_gain,
    policy_weight,
    frozen_weight,
    valid_lengths,
    pair_rows,
):
    rows, tokens_here = policy_stream.shape
    seq_len = tokens_here // valid_lengths.shape[0]
    seqs = valid_lengths.shape[0] // NY
    tokens = tokens_here // NY
    z_hi, core, y = lax.axis_index("zh"), lax.axis_index("c"), lax.axis_index("y")

    contexts = jnp.stack(
        [policy_context.reshape(NY, tokens, 128), frozen_context.reshape(NY, tokens, 128)], axis=1
    )
    contexts = lax.all_to_all(contexts, "y", 0, 0)
    contexts = contexts.transpose(1, 2, 0, 3).reshape(2 * tokens, NY * 128)
    contexts = lax.all_gather(contexts, "zl", axis=1, tiled=True)

    frozen_rows = rows_of_all_y(frozen_weight, core)
    policy_rows = rows_of_all_y(policy_weight, core)
    streams = jnp.stack(
        [
            s.reshape(rows, NY, tokens).transpose(1, 0, 2)
            for s in (policy_stream, frozen_stream, targets)
        ],
        axis=1,
    )
    streams = lax.all_to_all(streams, "y", 0, 0)
    streams = streams.reshape(NY, 3, 2, rows // 2, tokens)
    streams = [jnp.stack(own_first(streams[:, i], core)) for i in range(3)]
    gains = spread(jnp.stack([policy_gain, frozen_gain]), "y", NY)
    gains = gains.reshape(NY, 2, 2, rows // 2, 1)
    gains = jnp.concatenate([g for i in range(2) for g in own_first(gains[:, i], core)], axis=1)
    other_targets = swapped(streams[2], "c")
    contexts, frozen_rows, policy_rows, streams, gains, other_targets = lax.optimization_barrier(
        (contexts, frozen_rows, policy_rows, streams, gains, other_targets)
    )

    policy_hidden, stats, columns, other_columns = forward(
        core, contexts, policy_rows, frozen_rows, streams, gains
    )
    stats = jnp.sum(lax.all_to_all(stats, "zl", 0, 0), axis=0)
    other_hidden = swapped(policy_hidden, "c")
    other_columns = swapped(other_columns, "c")

    policy_scale = lax.rsqrt(stats[0] / D + epsilon)
    frozen_scale = lax.rsqrt(stats[2] / D + epsilon)
    policy_dotted = stats[1]
    gap_of_token = policy_scale * policy_dotted - frozen_scale * stats[3]
    lengths = lax.dynamic_slice_in_dim(valid_lengths, y * seqs, seqs, 0)
    positions = lax.broadcasted_iota(jnp.int32, (seqs, seq_len), 1)
    valid = (positions < lengths[:, None]).astype(jnp.float32)
    own_gaps = jnp.sum(gap_of_token.reshape(seqs, seq_len) * valid, axis=1)
    told = jnp.concatenate([own_gaps, policy_scale, policy_dotted, valid.reshape(-1)])
    other_told = swapped(told, "c")
    other_gaps, other_told = other_told[:seqs], other_told[seqs:].reshape(3, tokens)
    chip_gaps = jnp.where(
        core == 0, jnp.stack([own_gaps, other_gaps]), jnp.stack([other_gaps, own_gaps])
    )
    gaps = spread(chip_gaps, ("zh", "x", "y"), 2 * NX * NY)
    gaps, other_columns, other_hidden = lax.optimization_barrier(
        (gaps, other_columns, other_hidden)
    )
    gaps = gaps.reshape(2 * NX, NY, 2, seqs).transpose(0, 2, 1, 3).reshape(-1)

    total_seqs = gaps.shape[0]
    pair_count = pair_rows.shape[0]
    row_ids = lax.broadcasted_iota(jnp.int32, (pair_count, total_seqs), 1)
    signs = (row_ids == pair_rows[:, 0:1]).astype(jnp.float32) - (
        row_ids == pair_rows[:, 1:2]
    ).astype(jnp.float32)
    margins = beta_scale * jnp.sum(signs * gaps[None, :], axis=1)
    loss = jnp.sum(jax.nn.softplus(-margins))
    slopes = -jax.nn.sigmoid(-margins)

    policy_gain = gains[:, :2].T[:, :, None]

    def hidden_grad_of(core_of_tokens, scale, dotted, valid, gain, all_targets, all_hidden):
        own_ids = (
            ((lax.axis_index(("zh", "x")) * 2 + core_of_tokens) * NY + y) * seqs
            + lax.broadcasted_iota(jnp.int32, (1, seqs), 1)
        )
        own_chosen = (pair_rows[:, 0:1] == own_ids).astype(jnp.float32)
        own_rejected = (pair_rows[:, 1:2] == own_ids).astype(jnp.float32)
        coef = beta_scale * jnp.sum(slopes[:, None] * (own_chosen - own_rejected), axis=0)
        step_size = jnp.broadcast_to(coef[:, None], (seqs, seq_len)).reshape(tokens) * valid * scale
        correction = dotted * scale * scale / D
        grad = step_size * (gain * all_targets.astype(jnp.float32) - all_hidden * correction)
        grad = grad.astype(jnp.bfloat16)
        grad = jnp.where(core_of_tokens == 0, grad, grad[::-1]).reshape(2, NY, rows // 2, tokens)
        return grad.transpose(1, 0, 2, 3).reshape(NY * rows, tokens)

    own_grad = hidden_grad_of(
        core,
        policy_scale,
        policy_dotted,
        valid.reshape(-1),
        policy_gain,
        streams[2],
        policy_hidden,
    )
    other_grad = hidden_grad_of(
        1 - core, *other_told, policy_gain[::-1], other_targets, other_hidden
    )
    hidden_grad = jnp.concatenate([own_grad, other_grad], axis=1)
    columns = jnp.concatenate([columns, other_columns], axis=2)

    def grad_of(z_hi):
        piece = lax.dynamic_index_in_dim(columns, z_hi, 0, keepdims=False)
        return jnp.stack(
            [jnp.dot(hidden_grad, piece[i], preferred_element_type=jnp.float32) for i in range(NX)]
        )

    z_order = (1 - z_hi, z_hi)
    sums = []
    for z in z_order:
        grad = grad_of(z).astype(jnp.bfloat16).reshape(NX * NY, rows, 256)
        grad = lax.all_to_all(grad, ("x", "y"), 0, 0)
        sums.append(jnp.sum(grad.astype(jnp.float32), axis=0))
    weight_grad = sums[1] + swapped(sums[0], "zh")
    return (weight_grad, margins, loss)


def solution(mesh):
    dp, blk = ("zh", "x", "c"), ("y", "zl")
    fine = Mesh(mesh.devices.reshape(2, NX, 2, NY, NZ), dp + blk)
    placed = (
        P(dp, blk),
        P(dp, blk),
        P(blk, dp),
        P(blk, dp),
        P(blk, dp),
        P(blk),
        P(blk),
        P(blk, None),
        P(blk, None),
        P(dp),
        P(),
    )
    return jax.shard_map(
        shards, mesh=fine, in_specs=placed, out_specs=(P(blk, dp), P(), P()), check_vma=False
    )
```

time: 276 us -> 256 us (0.928)
  the two profiles are of different devices: /device:TPU:35 before, /device:TPU:6 now
where the time goes in v3:
time: 256 us; the launch traced here: 251 us
  waiting for transfers between devices  122 us (48%)
  starting transfers between devices  62 us (24%)
  local copies, waits for them, and re-layouts  16.7 us (7%)
  between operations  14.6 us (6%)
  blocking collectives  13.7 us (5%)
  Pallas kernels  9.5 us (4%)
  other arithmetic  8.79 us (3%)
  matrix products  3.68 us (1%)
    all_to_all x4, waiting for transfers between devices, spread(): lax.all_to_all(jnp.broadcast_to(value[None], (count,) + value.shape), axe...  68.3 us
    all_to_all x4, starting transfers between devices, spread(): lax.all_to_all(jnp.broadcast_to(value[None], (count,) + value.shape), axe...  25.4 us
    all_to_all x2, waiting for transfers between devices, shards(): grad = lax.all_to_all(grad, ('x', 'y'), 0, 0)  23.9 us
    ppermute x7, starting transfers between devices, swapped(): return lax.ppermute(value, axis, [(0, 1), (1, 0)])  15 us
    all_to_all x1, blocking collectives, shards(): contexts = lax.all_to_all(contexts, 'y', 0, 0)  13.7 us
    all_to_all x1, waiting for transfers between devices, shards(): streams = lax.all_to_all(streams, 'y', 0, 0)  12.8 us
    all_to_all x2, starting transfers between devices, shards(): grad = lax.all_to_all(grad, ('x', 'y'), 0, 0)  11.7 us
    pallas_call x1, Pallas kernels, forward(): pl.pallas_call(forward_step, grid=(NZ // 2,), in_specs=[pl.BlockSpec(memo...  9.5 us
  transfers between devices with their start and end apart: 16, of which 11 were waited for; matrix products, arithmetic and copies ran while one was open for 7% of the time, Pallas kernels for 0%

profile of v3, /device:TPU:6, one launch (start us, length us, event | category | flops | bytes accessed | tf_op | source)
XLA Modules:
  0.0 251.2 jit_solution(15624485056664956720)
XLA Ops:
  8.3 13.7 %all_to_all.45 = bf16[4,2,256,128]{3,2,1,0:T(8,128)(2,1)S(1)} all-to-all(bf16[4,2,256,128]{3,2,1,0:T(8,128)(2,1)S(1)} %pad_maximum_fusion.4), channel_id=1, replica_groups=mesh['zh'=2,'x'=4,'c'=2,'y'=4,'zl'=8] {'y'}, dimensions={0} | all-to-all | bytes 1048576 | tf_op jit(solution)/shard_map/all_to_all | solution.py:169
  26.5 3.6 %all-to-all-start.1 = ((bf16[4,72,4096]{2,1,0:T(8,128)(2,1)}), bf16[4,72,4096]{2,1,0:T(8,128)(2,1)S(1)}, u32[]{:S(2)}, u32[]{:S(2)}) async-start(bf16[4,72,4096]{2,1,0:T(8,128)(2,1)} %broadcast_in_dim.20), calls=%async_computation.1 | async-start | bytes 4718592 | tf_op jit(solution)/shard_map/all_to_all | solution.py:16
  30.9 27.4 %all-to-all-done.1 = bf16[4,72,4096]{2,1,0:T(8,128)(2,1)S(1)} async-done(((bf16[4,72,4096]{2,1,0:T(8,128)(2,1)}), bf16[4,72,4096]{2,1,0:T(8,128)(2,1)S(1)}, u32[]{:S(2)}, u32[]{:S(2)}) %all-to-all-start.1) | async-done | bytes 2359328 | tf_op jit(solution)/shard_map/all_to_all | solution.py:16
  60.3 4.7 %all-to-all-start.2 = ((bf16[4,72,4096]{2,1,0:T(8,128)(2,1)}), bf16[4,72,4096]{2,1,0:T(8,128)(2,1)}, u32[]{:S(2)}, u32[]{:S(2)}) async-start(bf16[4,72,4096]{2,1,0:T(8,128)(2,1)} %broadcast_in_dim.22), calls=%async_computation.2 | async-start | bytes 4718592 | tf_op jit(solution)/shard_map/all_to_all | solution.py:16
  67.1 25.3 %all-to-all-done.2 = bf16[4,72,4096]{2,1,0:T(8,128)(2,1)} async-done(((bf16[4,72,4096]{2,1,0:T(8,128)(2,1)}), bf16[4,72,4096]{2,1,0:T(8,128)(2,1)}, u32[]{:S(2)}, u32[]{:S(2)}) %all-to-all-start.2) | async-done | bytes 2359328 | tf_op jit(solution)/shard_map/all_to_all | solution.py:16
  94.9 3.2 %all-to-all-start.4 = ((f32[4,2,144]{2,1,0:T(2,128)}), f32[4,2,144]{2,1,0:T(2,128)S(1)}, u32[]{:S(2)}, u32[]{:S(2)}) async-start(f32[4,2,144]{2,1,0:T(2,128)} %broadcast_in_dim.23), calls=%async_computation.4 | async-start | bytes 16384 | tf_op jit(solution)/shard_map/all_to_all | solution.py:16
  100.6 2.9 %all-to-all-done.4 = f32[4,2,144]{2,1,0:T(2,128)S(1)} async-done(((f32[4,2,144]{2,1,0:T(2,128)}), f32[4,2,144]{2,1,0:T(2,128)S(1)}, u32[]{:S(2)}, u32[]{:S(2)}) %all-to-all-start.4) | async-done | bytes 4640 | tf_op jit(solution)/shard_map/all_to_all | solution.py:16
  103.5 3.5 %all-to-all-start.3 = ((bf16[4,3,144,256]{3,2,1,0:T(8,128)(2,1)}), bf16[4,3,144,256]{3,2,1,0:T(8,128)(2,1)S(1)}, u32[]{:S(2)}, u32[]{:S(2)}) async-start(bf16[4,3,144,256]{3,2,1,0:T(8,128)(2,1)} %copy.54), calls=%async_computation.3 | async-start | bytes 1769472 | tf_op jit(solution)/shard_map/all_to_all | solution.py:182
  107.6 12.8 %all-to-all-done.3 = bf16[4,3,144,256]{3,2,1,0:T(8,128)(2,1)S(1)} async-done(((bf16[4,3,144,256]{3,2,1,0:T(8,128)(2,1)}), bf16[4,3,144,256]{3,2,1,0:T(8,128)(2,1)S(1)}, u32[]{:S(2)}, u32[]{:S(2)}) %all-to-all-start.3) | async-done | bytes 884768 | tf_op jit(solution)/shard_map/all_to_all | solution.py:182
  124.1 6.3 %all-gather.2.cloned.1.call-done.context_ref = bf16[512,4096]{1,0:T(8,128)(2,1)} async-done(((bf16[512,512]{1,0:T(8,128)(2,1)}), bf16[512,4096]{1,0:T(8,128)(2,1)}) %all-gather.2.cloned.1.call-update) | async-done | bytes 4194320 | tf_op jit(solution)/shard_map/all_gather | solution.py:171
  131.2 9.5 %shard_map.130 = (f32[2,288,256]{2,1,0:T(8,128)}, f32[8,4,256]{2,1,0:T(4,128)}, bf16[2,4,256,256]{3,2,1,0:T(8,128)(2,1)}, bf16[2,4,256,256]{3,2,1,0:T(8,128)(2,1)}) custom-call(s32[1]{0:T(128)} %bitcast.2.core_ref, bf16[512,4096]{1,0:T(8,128)(2,1)} %all-gather.2.cloned.1.call-done.context_ref, bf16[288,4096]{1,0:T(8,128)(2,1)} %bitcast.9.policy_mine_ref, ...), custom_call_target="tpu_custom_call" | custom-call | flops 2415919104 | bytes 15728640 | tf_op jit(solution)/shard_map/pallas_call | solution.py:115
  140.7 6.3 %all-to-all-start.5 = ((f32[8,4,256]{2,1,0:T(4,128)}), f32[8,4,256]{2,1,0:T(4,128)S(1)}, u32[]{:S(2)}, u32[]{:S(2)}) async-start(f32[8,4,256]{2,1,0:T(4,128)} %get-tuple-element.29), calls=%async_computation.5 | async-start | bytes 65536 | tf_op jit(solution)/shard_map/all_to_all | solution.py:196
  147.2 2.1 collective-permute-start.4
  149.3 2.2 collective-permute-start.5
  151.5 6.2 %all-to-all-done.5 = f32[8,4,256]{2,1,0:T(4,128)S(1)} async-done(((f32[8,4,256]{2,1,0:T(4,128)}), f32[8,4,256]{2,1,0:T(4,128)S(1)}, u32[]{:S(2)}, u32[]{:S(2)}) %all-to-all-start.5) | async-done | bytes 32800 | tf_op jit(solution)/shard_map/all_to_all | solution.py:196
  161.8 13.8 %all-to-all-start.6 = ((f32[32,2,4]{2,1,0:T(2,128)}), f32[32,2,4]{2,1,0:T(2,128)S(1)}, u32[]{:S(2)}, u32[]{:S(2)}) async-start(f32[32,2,4]{2,1,0:T(2,128)} %broadcast_in_dim.24), calls=%async_computation.6 | async-start | bytes 65536 | tf_op jit(solution)/shard_map/all_to_all | solution.py:16
  175.6 2.4 constant_dynamic-update-slice_fusion.1
  178.1 12.7 %all-to-all-done.6 = f32[32,2,4]{2,1,0:T(2,128)S(1)} async-done(((f32[32,2,4]{2,1,0:T(2,128)}), f32[32,2,4]{2,1,0:T(2,128)S(1)}, u32[]{:S(2)}, u32[]{:S(2)}) %all-to-all-start.6) | async-done | bytes 1056 | tf_op jit(solution)/shard_map/all_to_all | solution.py:16
  197.6 5.8 %all-to-all-start.8 = ((bf16[16,144,256]{2,1,0:T(8,128)(2,1)}), bf16[16,144,256]{2,1,0:T(8,128)(2,1)S(1)}, u32[]{:S(2)}, u32[]{:S(2)}) async-start(bf16[16,144,256]{2,1,0:T(8,128)(2,1)} %bitcast.55), calls=%async_computation.8 | async-start | bytes 2359296 | tf_op jit(solution)/shard_map/all_to_all | solution.py:272
  207.0 12.2 %all-to-all-done.8 = bf16[16,144,256]{2,1,0:T(8,128)(2,1)S(1)} async-done(((bf16[16,144,256]{2,1,0:T(8,128)(2,1)}), bf16[16,144,256]{2,1,0:T(8,128)(2,1)S(1)}, u32[]{:S(2)}, u32[]{:S(2)}) %all-to-all-start.8) | async-done | bytes 1179680 | tf_op jit(solution)/shard_map/all_to_all | solution.py:272
  219.2 5.9 %all-to-all-start.7 = ((bf16[16,144,256]{2,1,0:T(8,128)(2,1)}), bf16[16,144,256]{2,1,0:T(8,128)(2,1)S(1)}, u32[]{:S(2)}, u32[]{:S(2)}) async-start(bf16[16,144,256]{2,1,0:T(8,128)(2,1)} %bitcast.46), calls=%async_computation.7 | async-start | bytes 2359296 | tf_op jit(solution)/shard_map/all_to_all | solution.py:272
  225.3 2.9 %collective-permute-start.6 = (f32[144,256]{1,0:T(8,128)S(1)}, f32[144,256]{1,0:T(8,128)S(1)}, u32[]{:S(2)}, u32[]{:S(2)}) collective-permute-start(f32[144,256]{1,0:T(8,128)S(1)} %convert_reduce_fusion), channel_id=1, source_target_pairs={{0,256},{256,0},{1,257},{257,1},{2,258},{258,2},{3,259},{259,3},{4... | collective-permute-start | bytes 442376 | tf_op jit(solution)/shard_map/ppermute | solution.py:20
  228.2 11.7 %all-to-all-done.7 = bf16[16,144,256]{2,1,0:T(8,128)(2,1)S(1)} async-done(((bf16[16,144,256]{2,1,0:T(8,128)(2,1)}), bf16[16,144,256]{2,1,0:T(8,128)(2,1)S(1)}, u32[]{:S(2)}, u32[]{:S(2)}) %all-to-all-start.7) | async-done | bytes 1179680 | tf_op jit(solution)/shard_map/all_to_all | solution.py:272
  240.1 3.5 %collective-permute-done.6 = f32[144,256]{1,0:T(8,128)S(1)} collective-permute-done((f32[144,256]{1,0:T(8,128)S(1)}, f32[144,256]{1,0:T(8,128)S(1)}, u32[]{:S(2)}, u32[]{:S(2)}) %collective-permute-start.6) | collective-permute-done | bytes 147488 | tf_op jit(solution)/shard_map/ppermute | solution.py:20
  (138 shorter events, 35.8 us)
Async XLA Ops:
  7.2 123.2 %all-gather.2.cloned.1.call-start = ((), (), s32[]{:S(2)}) async-start(), calls=%async_computation.9 | async-start | bytes 4718592 | tf_op jit(solution)/shard_map/all_gather | solution.py:171
  26.5 31.8 %all-to-all-start.1 = ((bf16[4,72,4096]{2,1,0:T(8,128)(2,1)}), bf16[4,72,4096]{2,1,0:T(8,128)(2,1)S(1)}, u32[]{:S(2)}, u32[]{:S(2)}) async-start(bf16[4,72,4096]{2,1,0:T(8,128)(2,1)} %broadcast_in_dim.20), calls=%async_computation.1 | async-start | bytes 4718592 | tf_op jit(solution)/shard_map/all_to_all | solution.py:16
  60.3 34.0 %copy-start.17 = (f32[144]{0:T(256)S(1)}, f32[144]{0:T(256)}, u32[]{:S(2)}) copy-start(f32[144]{0:T(256)} %param.17) | copy-start | bytes 1732
  60.3 34.0 %copy-start.18 = (f32[144]{0:T(256)S(1)}, f32[144]{0:T(256)}, u32[]{:S(2)}) copy-start(f32[144]{0:T(256)} %param.16) | copy-start | bytes 1732
  60.3 37.9 %copy-start.9 = (bf16[144,1024]{1,0:T(8,128)(2,1)S(1)}, bf16[144,1024]{1,0:T(8,128)(2,1)}, u32[]{:S(2)}) copy-start(bf16[144,1024]{1,0:T(8,128)(2,1)} %param.13) | copy-start | bytes 884740
  60.3 38.1 %copy-start.10 = (bf16[144,1024]{1,0:T(8,128)(2,1)S(1)}, bf16[144,1024]{1,0:T(8,128)(2,1)}, u32[]{:S(2)}) copy-start(bf16[144,1024]{1,0:T(8,128)(2,1)} %param.14) | copy-start | bytes 884740
  60.3 32.1 %all-to-all-start.2 = ((bf16[4,72,4096]{2,1,0:T(8,128)(2,1)}), bf16[4,72,4096]{2,1,0:T(8,128)(2,1)}, u32[]{:S(2)}, u32[]{:S(2)}) async-start(bf16[4,72,4096]{2,1,0:T(8,128)(2,1)} %broadcast_in_dim.22), calls=%async_computation.2 | async-start | bytes 4718592 | tf_op jit(solution)/shard_map/all_to_all | solution.py:16
  65.0 33.7 %copy-start.11 = (bf16[144,1024]{1,0:T(8,128)(2,1)S(1)}, bf16[144,1024]{1,0:T(8,128)(2,1)}, u32[]{:S(2)}) copy-start(bf16[144,1024]{1,0:T(8,128)(2,1)} %param.15) | copy-start | bytes 884740
  65.0 59.1 %collective-permute-start = (bf16[288,4096]{1,0:T(8,128)(2,1)S(1)}, bf16[288,4096]{1,0:T(8,128)(2,1)}, u32[]{:S(2)}, u32[]{:S(2)}) collective-permute-start(bf16[288,4096]{1,0:T(8,128)(2,1)S(1)} %bitcast.104), channel_id=1, source_target_pairs={{0,32},{32,0},{1,33},{33,1},{2,34},{34,2},{3,35},{35,3},{4,36},{36... | collective-permute-start | bytes 7077896 | tf_op jit(solution)/shard_map/ppermute | solution.py:20
  92.4 31.8 %collective-permute-start.1 = (bf16[288,4096]{1,0:T(8,128)(2,1)}, bf16[288,4096]{1,0:T(8,128)(2,1)}, u32[]{:S(2)}, u32[]{:S(2)}) collective-permute-start(bf16[288,4096]{1,0:T(8,128)(2,1)} %bitcast.9.policy_mine_ref), channel_id=1, source_target_pairs={{0,32},{32,0},{1,33},{33,1},{2,34},{34,2},{3,35},{35,3},{4,36},{36... | collective-permute-start | bytes 7077896 | tf_op jit(solution)/shard_map/ppermute | solution.py:20
  94.9 8.5 %all-to-all-start.4 = ((f32[4,2,144]{2,1,0:T(2,128)}), f32[4,2,144]{2,1,0:T(2,128)S(1)}, u32[]{:S(2)}, u32[]{:S(2)}) async-start(f32[4,2,144]{2,1,0:T(2,128)} %broadcast_in_dim.23), calls=%async_computation.4 | async-start | bytes 16384 | tf_op jit(solution)/shard_map/all_to_all | solution.py:16
  103.5 17.0 %all-to-all-start.3 = ((bf16[4,3,144,256]{3,2,1,0:T(8,128)(2,1)}), bf16[4,3,144,256]{3,2,1,0:T(8,128)(2,1)S(1)}, u32[]{:S(2)}, u32[]{:S(2)}) async-start(bf16[4,3,144,256]{3,2,1,0:T(8,128)(2,1)} %copy.54), calls=%async_computation.3 | async-start | bytes 1769472 | tf_op jit(solution)/shard_map/all_to_all | solution.py:182
  120.7 3.5 %collective-permute-start.2 = (bf16[2,288,256]{2,1,0:T(8,128)(2,1)S(1)}, bf16[2,288,256]{2,1,0:T(8,128)(2,1)S(1)}, u32[]{:S(2)}, u32[]{:S(2)}) collective-permute-start(bf16[2,288,256]{2,1,0:T(8,128)(2,1)S(1)} %pad_maximum_fusion.7.targets_ref), channel_id=1, source_target_pairs={{0,32},{32,0},{1,33},{33,1},{2,34},{34,2},{3,35},{35,3},{4,36},{36... | collective-permute-start | bytes 884744 | tf_op jit(solution)/shard_map/ppermute | solution.py:20
  131.2 15.8 %copy-start.16 = (s32[128,2]{0,1:T(2,128)S(1)}, s32[128,2]{0,1:T(2,128)}, u32[]{:S(2)}) copy-start(s32[128,2]{0,1:T(2,128)} %param.21) | copy-start | bytes 3076
  140.7 17.0 %all-to-all-start.5 = ((f32[8,4,256]{2,1,0:T(4,128)}), f32[8,4,256]{2,1,0:T(4,128)S(1)}, u32[]{:S(2)}, u32[]{:S(2)}) async-start(f32[8,4,256]{2,1,0:T(4,128)} %get-tuple-element.29), calls=%async_computation.5 | async-start | bytes 65536 | tf_op jit(solution)/shard_map/all_to_all | solution.py:196
  147.2 43.7 %collective-permute-start.4 = (bf16[2,4,256,256]{3,2,1,0:T(8,128)(2,1)}, bf16[2,4,256,256]{3,2,1,0:T(8,128)(2,1)S(1)}, u32[]{:S(2)}, u32[]{:S(2)}) collective-permute-start(bf16[2,4,256,256]{3,2,1,0:T(8,128)(2,1)} %get-tuple-element.30), channel_id=1, source_target_pairs={{0,32},{32,0},{1,33},{33,1},{2,34},{34,2},{3,35},{35,3},{4,36},{36... | collective-permute-start | bytes 3145736 | tf_op jit(solution)/shard_map/ppermute | solution.py:20
  149.3 41.5 %collective-permute-start.5 = (f32[2,288,256]{2,1,0:T(8,128)}, f32[2,288,256]{2,1,0:T(8,128)S(1)}, u32[]{:S(2)}, u32[]{:S(2)}) collective-permute-start(f32[2,288,256]{2,1,0:T(8,128)} %get-tuple-element.31), channel_id=1, source_target_pairs={{0,32},{32,0},{1,33},{33,1},{2,34},{34,2},{3,35},{35,3},{4,36},{36... | collective-permute-start | bytes 1769480 | tf_op jit(solution)/shard_map/ppermute | solution.py:20
  158.1 3.1 %collective-permute-start.3 = (f32[772]{0:T(1024)S(1)}, f32[772]{0:T(1024)S(1)}, u32[]{:S(2)}, u32[]{:S(2)}) collective-permute-start(f32[772]{0:T(1024)S(1)} %pad_maximum_fusion.9), channel_id=1, source_target_pairs={{0,32},{32,0},{1,33},{33,1},{2,34},{34,2},{3,35},{35,3},{4,36},{36... | collective-permute-start | bytes 9272 | tf_op jit(solution)/shard_map/ppermute | solution.py:20
  161.8 30.8 %copy-start.2 = (bf16[2,288,256]{2,1,0:T(8,128)(2,1)S(1)}, bf16[2,288,256]{2,1,0:T(8,128)(2,1)}, u32[]{:S(2)}) copy-start(bf16[2,288,256]{2,1,0:T(8,128)(2,1)} %copy-done.1) | copy-start | bytes 884740
  161.8 30.8 %copy-start.3 = (f32[2,288,256]{2,1,0:T(8,128)S(1)}, f32[2,288,256]{2,1,0:T(8,128)}, u32[]{:S(2)}) copy-start(f32[2,288,256]{2,1,0:T(8,128)} %get-tuple-element.31) | copy-start | bytes 1769476
  161.8 29.0 %all-to-all-start.6 = ((f32[32,2,4]{2,1,0:T(2,128)}), f32[32,2,4]{2,1,0:T(2,128)S(1)}, u32[]{:S(2)}, u32[]{:S(2)}) async-start(f32[32,2,4]{2,1,0:T(2,128)} %broadcast_in_dim.24), calls=%async_computation.6 | async-start | bytes 65536 | tf_op jit(solution)/shard_map/all_to_all | solution.py:16
  197.6 21.6 %all-to-all-start.8 = ((bf16[16,144,256]{2,1,0:T(8,128)(2,1)}), bf16[16,144,256]{2,1,0:T(8,128)(2,1)S(1)}, u32[]{:S(2)}, u32[]{:S(2)}) async-start(bf16[16,144,256]{2,1,0:T(8,128)(2,1)} %bitcast.55), calls=%async_computation.8 | async-start | bytes 2359296 | tf_op jit(solution)/shard_map/all_to_all | solution.py:272
  219.2 20.7 %all-to-all-start.7 = ((bf16[16,144,256]{2,1,0:T(8,128)(2,1)}), bf16[16,144,256]{2,1,0:T(8,128)(2,1)S(1)}, u32[]{:S(2)}, u32[]{:S(2)}) async-start(bf16[16,144,256]{2,1,0:T(8,128)(2,1)} %bitcast.46), calls=%async_computation.7 | async-start | bytes 2359296 | tf_op jit(solution)/shard_map/all_to_all | solution.py:272
  225.3 18.3 %collective-permute-start.6 = (f32[144,256]{1,0:T(8,128)S(1)}, f32[144,256]{1,0:T(8,128)S(1)}, u32[]{:S(2)}, u32[]{:S(2)}) collective-permute-start(f32[144,256]{1,0:T(8,128)S(1)} %convert_reduce_fusion), channel_id=1, source_target_pairs={{0,256},{256,0},{1,257},{257,1},{2,258},{258,2},{3,259},{259,3},{4... | collective-permute-start | bytes 442376 | tf_op jit(solution)/shard_map/ppermute | solution.py:20
  (13 other events, 43.0 us)
Sparse Core Ops, SparseCore 0:
  23.5 106.8 all-gather.1

commit v4 on v3

--- a/solution.py
+++ b/solution.py
@@ -46,6 +46,7 @@
     frozen_stream_ref,
     targets_ref,
     gains_ref,
+    valid_ref,
     hidden_ref,
     stats_ref,
     own_columns_ref,
@@ -97,11 +98,14 @@
                 terms = (hidden * hidden, hidden * (gain * target))
                 for i, term in enumerate(terms):
                     totals[2 * model + i] += jnp.sum(term, axis=0, keepdims=True)
-        for i in range(4):
-            stats_ref[:, i : i + 1, :] = jnp.broadcast_to(totals[i][None], (NZ, 1, tokens))
-
-
-def forward(core, contexts, policy_rows, frozen_rows, streams, gains):
+        totals.append(valid_ref[...])
+        for i in range(5):
+            stats_ref[:, i : i + 1, :] = jnp.broadcast_to(
+                totals[i][None], (2 * NZ, 1, tokens)
+            )
+
+
+def forward(core, contexts, policy_rows, frozen_rows, streams, gains, valid):
     half_rows, features = policy_rows[0].shape
     tokens = contexts.shape[0] // 2
     depth = features // (NZ // 2)
@@ -126,11 +130,12 @@
             whole(*block),
             whole(*block),
             whole(half_rows, 4),
+            whole(1, tokens),
         ],
-        out_specs=[whole(*block), whole(NZ, 4, tokens), whole(*columns), whole(*columns)],
+        out_specs=[whole(*block), whole(2 * NZ, 5, tokens), whole(*columns), whole(*columns)],
         out_shape=[
             jax.ShapeDtypeStruct(block, jnp.float32),
-            jax.ShapeDtypeStruct((NZ, 4, tokens), jnp.float32),
+            jax.ShapeDtypeStruct((2 * NZ, 5, tokens), jnp.float32),
             jax.ShapeDtypeStruct(columns, jnp.bfloat16),
             jax.ShapeDtypeStruct(columns, jnp.bfloat16),
         ],
@@ -141,7 +146,7 @@
             bytes_accessed=2 * features * (4 * half_rows + 3 * tokens),
             transcendentals=0,
         ),
-    )(core[None], contexts, *policy_rows, *frozen_rows, *streams, gains)
+    )(core[None], contexts, *policy_rows, *frozen_rows, *streams, gains, valid)
 
 
 def shards(
@@ -186,36 +191,39 @@
     gains = gains.reshape(NY, 2, 2, rows // 2, 1)
     gains = jnp.concatenate([g for i in range(2) for g in own_first(gains[:, i], core)], axis=1)
     other_targets = swapped(streams[2], "c")
-    contexts, frozen_rows, policy_rows, streams, gains, other_targets = lax.optimization_barrier(
-        (contexts, frozen_rows, policy_rows, streams, gains, other_targets)
-    )
-
+    lengths = lax.dynamic_slice_in_dim(valid_lengths, y * seqs, seqs, 0)
+    positions = lax.broadcasted_iota(jnp.int32, (seqs, seq_len), 1)
+    valid = (positions < lengths[:, None]).astype(jnp.float32).reshape(1, tokens)
+    contexts, frozen_rows, policy_rows, streams, gains, other_targets, valid = (
+        lax.optimization_barrier(
+            (contexts, frozen_rows, policy_rows, streams, gains, other_targets, valid)
+        )
+    )
     policy_hidden, stats, columns, other_columns = forward(
-        core, contexts, policy_rows, frozen_rows, streams, gains
-    )
-    stats = jnp.sum(lax.all_to_all(stats, "zl", 0, 0), axis=0)
+        core, contexts, policy_rows, frozen_rows, streams, gains, valid
+    )
+    stats = lax.all_to_all(stats, ("zh", "zl"), 0, 0).reshape(2, NZ, 5, tokens)
+    valid = stats[:, 0, 4]
+    stats = jnp.sum(stats[:, :, :4], axis=1)
     other_hidden = swapped(policy_hidden, "c")
     other_columns = swapped(other_columns, "c")
 
-    policy_scale = lax.rsqrt(stats[0] / D + epsilon)
-    frozen_scale = lax.rsqrt(stats[2] / D + epsilon)
-    policy_dotted = stats[1]
-    gap_of_token = policy_scale * policy_dotted - frozen_scale * stats[3]
-    lengths = lax.dynamic_slice_in_dim(valid_lengths, y * seqs, seqs, 0)
-    positions = lax.broadcasted_iota(jnp.int32, (seqs, seq_len), 1)
-    valid = (positions < lengths[:, None]).astype(jnp.float32)
-    own_gaps = jnp.sum(gap_of_token.reshape(seqs, seq_len) * valid, axis=1)
-    told = jnp.concatenate([own_gaps, policy_scale, policy_dotted, valid.reshape(-1)])
+    scales = lax.rsqrt(stats[:, 0::2] / D + epsilon)
+    gap_of_token = scales[:, 0] * stats[:, 1] - scales[:, 1] * stats[:, 3]
+    own_gaps = jnp.sum((gap_of_token * valid).reshape(2 * seqs, seq_len), axis=1)
+    scalars = jnp.stack([scales[:, 0], stats[:, 1], valid], axis=1)
+    scalars = lax.dynamic_index_in_dim(scalars, z_hi, 0, keepdims=False)
+    told = jnp.concatenate([own_gaps, scalars.reshape(-1)])
     other_told = swapped(told, "c")
-    other_gaps, other_told = other_told[:seqs], other_told[seqs:].reshape(3, tokens)
+    other_gaps, other_told = other_told[: 2 * seqs], other_told[2 * seqs :].reshape(3, tokens)
     chip_gaps = jnp.where(
         core == 0, jnp.stack([own_gaps, other_gaps]), jnp.stack([other_gaps, own_gaps])
     )
-    gaps = spread(chip_gaps, ("zh", "x", "y"), 2 * NX * NY)
+    gaps = spread(chip_gaps, ("x", "y"), NX * NY)
     gaps, other_columns, other_hidden = lax.optimization_barrier(
         (gaps, other_columns, other_hidden)
     )
-    gaps = gaps.reshape(2 * NX, NY, 2, seqs).transpose(0, 2, 1, 3).reshape(-1)
+    gaps = gaps.reshape(NX, NY, 2, 2, seqs).transpose(3, 0, 2, 1, 4).reshape(-1)
 
     total_seqs = gaps.shape[0]
     pair_count = pair_rows.shape[0]
@@ -244,15 +252,7 @@
         grad = jnp.where(core_of_tokens == 0, grad, grad[::-1]).reshape(2, NY, rows // 2, tokens)
         return grad.transpose(1, 0, 2, 3).reshape(NY * rows, tokens)
 
-    own_grad = hidden_grad_of(
-        core,
-        policy_scale,
-        policy_dotted,
-        valid.reshape(-1),
-        policy_gain,
-        streams[2],
-        policy_hidden,
-    )
+    own_grad = hidden_grad_of(core, *scalars, policy_gain, streams[2], policy_hidden)
     other_grad = hidden_grad_of(
         1 - core, *other_told, policy_gain[::-1], other_targets, other_hidden
     )

time: 256 us -> 244 us (0.953)
  waiting for transfers between devices: 122 us -> 113 us
  starting transfers between devices: 62 us -> 59 us
    all_to_all x4, waiting for transfers between devices: 68.3 us -> 58.8 us  [spread(): lax.all_to_all(jnp.broadcast_to(value[None], (count,) + value.shape), axe...]
    all_to_all x4, starting transfers between devices: 25.4 us -> 16.9 us  [spread(): lax.all_to_all(jnp.broadcast_to(value[None], (count,) + value.shape), axe...]
    all_to_all x1, waiting for transfers between devices: 6.18 us -> 9.64 us  [shards(): stats = lax.all_to_all(stats, ('zh', 'zl'), 0, 0).reshape(2, NZ, 5, tokens)]
    ppermute x7, starting transfers between devices: 15 us -> 17.8 us  [swapped(): return lax.ppermute(value, axis, [(0, 1), (1, 0)])]
    all_to_all x2, waiting for transfers between devices: 23.9 us -> 21.1 us  [shards(): grad = lax.all_to_all(grad, ('x', 'y'), 0, 0)]
    all_to_all x1, starting transfers between devices: 6.34 us -> 9.04 us  [shards(): stats = lax.all_to_all(stats, ('zh', 'zl'), 0, 0).reshape(2, NZ, 5, tokens)]
  transfers between devices with their start and end apart: 16 -> 16, of which waited for: 11 -> 11; matrix products, arithmetic and copies ran while one was open for 7% -> 8% of each run, Pallas kernels for 0% -> 0%
where the time goes in v4:
time: 244 us; the launch traced here: 240 us
  waiting for transfers between devices  113 us (46%)
  starting transfers between devices  59 us (24%)
  local copies, waits for them, and re-layouts  17.4 us (7%)
  between operations  14.6 us (6%)
  blocking collectives  13.7 us (6%)
  Pallas kernels  9.54 us (4%)
  other arithmetic  8.67 us (4%)
  matrix products  3.68 us (2%)
    all_to_all x4, waiting for transfers between devices, spread(): lax.all_to_all(jnp.broadcast_to(value[None], (count,) + value.shape), axe...  58.8 us
    all_to_all x2, waiting for transfers between devices, shards(): grad = lax.all_to_all(grad, ('x', 'y'), 0, 0)  21.1 us
    ppermute x7, starting transfers between devices, swapped(): return lax.ppermute(value, axis, [(0, 1), (1, 0)])  17.8 us
    all_to_all x4, starting transfers between devices, spread(): lax.all_to_all(jnp.broadcast_to(value[None], (count,) + value.shape), axe...  16.9 us
    all_to_all x1, blocking collectives, shards(): contexts = lax.all_to_all(contexts, 'y', 0, 0)  13.7 us
    all_to_all x1, waiting for transfers between devices, shards(): streams = lax.all_to_all(streams, 'y', 0, 0)  12.2 us
    all_to_all x2, starting transfers between devices, shards(): grad = lax.all_to_all(grad, ('x', 'y'), 0, 0)  11.7 us
    all_to_all x1, waiting for transfers between devices, shards(): stats = lax.all_to_all(stats, ('zh', 'zl'), 0, 0).reshape(2, NZ, 5, tokens)  9.64 us
  transfers between devices with their start and end apart: 16, of which 11 were waited for; matrix products, arithmetic and copies ran while one was open for 8% of the time, Pallas kernels for 0%

profile of v4, /device:TPU:6, one launch (start us, length us, event | category | flops | bytes accessed | tf_op | source)
XLA Modules:
  0.0 239.9 jit_solution(2862083539858770471)
XLA Ops:
  8.3 13.7 %all_to_all.45 = bf16[4,2,256,128]{3,2,1,0:T(8,128)(2,1)S(1)} all-to-all(bf16[4,2,256,128]{3,2,1,0:T(8,128)(2,1)S(1)} %pad_maximum_fusion.4), channel_id=1, replica_groups=mesh['zh'=2,'x'=4,'c'=2,'y'=4,'zl'=8] {'y'}, dimensions={0} | all-to-all | bytes 1048576 | tf_op jit(solution)/shard_map/all_to_all | solution.py:174
  26.5 3.6 %all-to-all-start.1 = ((bf16[4,72,4096]{2,1,0:T(8,128)(2,1)}), bf16[4,72,4096]{2,1,0:T(8,128)(2,1)S(1)}, u32[]{:S(2)}, u32[]{:S(2)}) async-start(bf16[4,72,4096]{2,1,0:T(8,128)(2,1)} %broadcast_in_dim.20), calls=%async_computation.1 | async-start | bytes 4718592 | tf_op jit(solution)/shard_map/all_to_all | solution.py:16
  30.9 27.4 %all-to-all-done.1 = bf16[4,72,4096]{2,1,0:T(8,128)(2,1)S(1)} async-done(((bf16[4,72,4096]{2,1,0:T(8,128)(2,1)}), bf16[4,72,4096]{2,1,0:T(8,128)(2,1)S(1)}, u32[]{:S(2)}, u32[]{:S(2)}) %all-to-all-start.1) | async-done | bytes 2359328 | tf_op jit(solution)/shard_map/all_to_all | solution.py:16
  60.3 4.7 %all-to-all-start.2 = ((bf16[4,72,4096]{2,1,0:T(8,128)(2,1)}), bf16[4,72,4096]{2,1,0:T(8,128)(2,1)}, u32[]{:S(2)}, u32[]{:S(2)}) async-start(bf16[4,72,4096]{2,1,0:T(8,128)(2,1)} %broadcast_in_dim.22), calls=%async_computation.2 | async-start | bytes 4718592 | tf_op jit(solution)/shard_map/all_to_all | solution.py:16
  67.1 25.3 %all-to-all-done.2 = bf16[4,72,4096]{2,1,0:T(8,128)(2,1)} async-done(((bf16[4,72,4096]{2,1,0:T(8,128)(2,1)}), bf16[4,72,4096]{2,1,0:T(8,128)(2,1)}, u32[]{:S(2)}, u32[]{:S(2)}) %all-to-all-start.2) | async-done | bytes 2359328 | tf_op jit(solution)/shard_map/all_to_all | solution.py:16
  95.0 3.2 %all-to-all-start.4 = ((f32[4,2,144]{2,1,0:T(2,128)}), f32[4,2,144]{2,1,0:T(2,128)S(1)}, u32[]{:S(2)}, u32[]{:S(2)}) async-start(f32[4,2,144]{2,1,0:T(2,128)} %broadcast_in_dim.23), calls=%async_computation.4 | async-start | bytes 16384 | tf_op jit(solution)/shard_map/all_to_all | solution.py:16
  100.7 2.8 %all-to-all-done.4 = f32[4,2,144]{2,1,0:T(2,128)S(1)} async-done(((f32[4,2,144]{2,1,0:T(2,128)}), f32[4,2,144]{2,1,0:T(2,128)S(1)}, u32[]{:S(2)}, u32[]{:S(2)}) %all-to-all-start.4) | async-done | bytes 4640 | tf_op jit(solution)/shard_map/all_to_all | solution.py:16
  103.5 3.5 %all-to-all-start.3 = ((bf16[4,3,144,256]{3,2,1,0:T(8,128)(2,1)}), bf16[4,3,144,256]{3,2,1,0:T(8,128)(2,1)S(1)}, u32[]{:S(2)}, u32[]{:S(2)}) async-start(bf16[4,3,144,256]{3,2,1,0:T(8,128)(2,1)} %copy.55), calls=%async_computation.3 | async-start | bytes 1769472 | tf_op jit(solution)/shard_map/all_to_all | solution.py:187
  108.4 12.2 %all-to-all-done.3 = bf16[4,3,144,256]{3,2,1,0:T(8,128)(2,1)S(1)} async-done(((bf16[4,3,144,256]{3,2,1,0:T(8,128)(2,1)}), bf16[4,3,144,256]{3,2,1,0:T(8,128)(2,1)S(1)}, u32[]{:S(2)}, u32[]{:S(2)}) %all-to-all-start.3) | async-done | bytes 884768 | tf_op jit(solution)/shard_map/all_to_all | solution.py:187
  124.2 6.2 %all-gather.2.cloned.1.call-done.context_ref = bf16[512,4096]{1,0:T(8,128)(2,1)} async-done(((bf16[512,512]{1,0:T(8,128)(2,1)}), bf16[512,4096]{1,0:T(8,128)(2,1)}) %all-gather.2.cloned.1.call-update) | async-done | bytes 4194320 | tf_op jit(solution)/shard_map/all_gather | solution.py:176
  131.2 9.5 %shard_map.130 = (f32[2,288,256]{2,1,0:T(8,128)}, f32[16,5,256]{2,1,0:T(8,128)}, bf16[2,4,256,256]{3,2,1,0:T(8,128)(2,1)}, bf16[2,4,256,256]{3,2,1,0:T(8,128)(2,1)}) custom-call(s32[1]{0:T(128)} %bitcast.2.core_ref, bf16[512,4096]{1,0:T(8,128)(2,1)} %all-gather.2.cloned.1.call-done.context_ref, bf16[288,4096]{1,0:T(8,128)(2,1)} %bitcast.9.policy_mine_ref, ...), custom_call_target="tpu_custom_call" | custom-call | flops 2415919104 | bytes 15728640 | tf_op jit(solution)/shard_map/pallas_call | solution.py:119
  140.8 9.0 %all-to-all-start.5 = ((f32[16,5,256]{2,1,0:T(8,128)}), f32[16,5,256]{2,1,0:T(8,128)S(1)}, u32[]{:S(2)}, u32[]{:S(2)}) async-start(f32[16,5,256]{2,1,0:T(8,128)} %get-tuple-element.31), calls=%async_computation.5 | async-start | bytes 262144 | tf_op jit(solution)/shard_map/all_to_all | solution.py:205
  149.9 2.1 collective-permute-start.4
  152.0 2.2 collective-permute-start.5
  154.2 9.6 %all-to-all-done.5 = f32[16,5,256]{2,1,0:T(8,128)S(1)} async-done(((f32[16,5,256]{2,1,0:T(8,128)}), f32[16,5,256]{2,1,0:T(8,128)S(1)}, u32[]{:S(2)}, u32[]{:S(2)}) %all-to-all-start.5) | async-done | bytes 81952 | tf_op jit(solution)/shard_map/all_to_all | solution.py:205
  168.0 5.4 %all-to-all-start.6 = ((f32[16,2,8]{2,1,0:T(2,128)}), f32[16,2,8]{2,1,0:T(2,128)S(1)}, u32[]{:S(2)}, u32[]{:S(2)}) async-start(f32[16,2,8]{2,1,0:T(2,128)} %broadcast_in_dim.24), calls=%async_computation.6 | async-start | bytes 32768 | tf_op jit(solution)/shard_map/all_to_all | solution.py:16
  173.4 2.3 constant_dynamic-update-slice_fusion.1
  175.8 3.2 %all-to-all-done.6 = f32[16,2,8]{2,1,0:T(2,128)S(1)} async-done(((f32[16,2,8]{2,1,0:T(2,128)}), f32[16,2,8]{2,1,0:T(2,128)S(1)}, u32[]{:S(2)}, u32[]{:S(2)}) %all-to-all-start.6) | async-done | bytes 1056 | tf_op jit(solution)/shard_map/all_to_all | solution.py:16
  185.8 5.8 %all-to-all-start.8 = ((bf16[16,144,256]{2,1,0:T(8,128)(2,1)}), bf16[16,144,256]{2,1,0:T(8,128)(2,1)S(1)}, u32[]{:S(2)}, u32[]{:S(2)}) async-start(bf16[16,144,256]{2,1,0:T(8,128)(2,1)} %bitcast.56), calls=%async_computation.8 | async-start | bytes 2359296 | tf_op jit(solution)/shard_map/all_to_all | solution.py:272
  195.2 12.2 %all-to-all-done.8 = bf16[16,144,256]{2,1,0:T(8,128)(2,1)S(1)} async-done(((bf16[16,144,256]{2,1,0:T(8,128)(2,1)}), bf16[16,144,256]{2,1,0:T(8,128)(2,1)S(1)}, u32[]{:S(2)}, u32[]{:S(2)}) %all-to-all-start.8) | async-done | bytes 1179680 | tf_op jit(solution)/shard_map/all_to_all | solution.py:272
  207.4 5.9 %all-to-all-start.7 = ((bf16[16,144,256]{2,1,0:T(8,128)(2,1)}), bf16[16,144,256]{2,1,0:T(8,128)(2,1)S(1)}, u32[]{:S(2)}, u32[]{:S(2)}) async-start(bf16[16,144,256]{2,1,0:T(8,128)(2,1)} %bitcast.47), calls=%async_computation.7 | async-start | bytes 2359296 | tf_op jit(solution)/shard_map/all_to_all | solution.py:272
  213.5 5.7 %collective-permute-start.6 = (f32[144,256]{1,0:T(8,128)S(1)}, f32[144,256]{1,0:T(8,128)S(1)}, u32[]{:S(2)}, u32[]{:S(2)}) collective-permute-start(f32[144,256]{1,0:T(8,128)S(1)} %convert_reduce_fusion), channel_id=1, source_target_pairs={{0,256},{256,0},{1,257},{257,1},{2,258},{258,2},{3,259},{259,3},{4... | collective-permute-start | bytes 442376 | tf_op jit(solution)/shard_map/ppermute | solution.py:20
  219.2 8.9 %all-to-all-done.7 = bf16[16,144,256]{2,1,0:T(8,128)(2,1)S(1)} async-done(((bf16[16,144,256]{2,1,0:T(8,128)(2,1)}), bf16[16,144,256]{2,1,0:T(8,128)(2,1)S(1)}, u32[]{:S(2)}, u32[]{:S(2)}) %all-to-all-start.7) | async-done | bytes 1179680 | tf_op jit(solution)/shard_map/all_to_all | solution.py:272
  228.3 4.0 %collective-permute-done.6 = f32[144,256]{1,0:T(8,128)S(1)} collective-permute-done((f32[144,256]{1,0:T(8,128)S(1)}, f32[144,256]{1,0:T(8,128)S(1)}, u32[]{:S(2)}, u32[]{:S(2)}) %collective-permute-start.6) | collective-permute-done | bytes 147488 | tf_op jit(solution)/shard_map/ppermute | solution.py:20
  (145 shorter events, 36.5 us)
Async XLA Ops:
  7.2 123.3 %all-gather.2.cloned.1.call-start = ((), (), s32[]{:S(2)}) async-start(), calls=%async_computation.9 | async-start | bytes 4718592 | tf_op jit(solution)/shard_map/all_gather | solution.py:176
  26.5 31.8 %all-to-all-start.1 = ((bf16[4,72,4096]{2,1,0:T(8,128)(2,1)}), bf16[4,72,4096]{2,1,0:T(8,128)(2,1)S(1)}, u32[]{:S(2)}, u32[]{:S(2)}) async-start(bf16[4,72,4096]{2,1,0:T(8,128)(2,1)} %broadcast_in_dim.20), calls=%async_computation.1 | async-start | bytes 4718592 | tf_op jit(solution)/shard_map/all_to_all | solution.py:16
  60.3 34.0 %copy-start.17 = (f32[144]{0:T(256)S(1)}, f32[144]{0:T(256)}, u32[]{:S(2)}) copy-start(f32[144]{0:T(256)} %param.17) | copy-start | bytes 1732
  60.3 34.0 %copy-start.18 = (f32[144]{0:T(256)S(1)}, f32[144]{0:T(256)}, u32[]{:S(2)}) copy-start(f32[144]{0:T(256)} %param.16) | copy-start | bytes 1732
  60.3 37.9 %copy-start.9 = (bf16[144,1024]{1,0:T(8,128)(2,1)S(1)}, bf16[144,1024]{1,0:T(8,128)(2,1)}, u32[]{:S(2)}) copy-start(bf16[144,1024]{1,0:T(8,128)(2,1)} %param.13) | copy-start | bytes 884740
  60.3 38.1 %copy-start.10 = (bf16[144,1024]{1,0:T(8,128)(2,1)S(1)}, bf16[144,1024]{1,0:T(8,128)(2,1)}, u32[]{:S(2)}) copy-start(bf16[144,1024]{1,0:T(8,128)(2,1)} %param.14) | copy-start | bytes 884740
  60.3 32.1 %all-to-all-start.2 = ((bf16[4,72,4096]{2,1,0:T(8,128)(2,1)}), bf16[4,72,4096]{2,1,0:T(8,128)(2,1)}, u32[]{:S(2)}, u32[]{:S(2)}) async-start(bf16[4,72,4096]{2,1,0:T(8,128)(2,1)} %broadcast_in_dim.22), calls=%async_computation.2 | async-start | bytes 4718592 | tf_op jit(solution)/shard_map/all_to_all | solution.py:16
  65.0 33.7 %copy-start.11 = (bf16[144,1024]{1,0:T(8,128)(2,1)S(1)}, bf16[144,1024]{1,0:T(8,128)(2,1)}, u32[]{:S(2)}) copy-start(bf16[144,1024]{1,0:T(8,128)(2,1)} %param.15) | copy-start | bytes 884740
  65.0 59.1 %collective-permute-start = (bf16[288,4096]{1,0:T(8,128)(2,1)S(1)}, bf16[288,4096]{1,0:T(8,128)(2,1)}, u32[]{:S(2)}, u32[]{:S(2)}) collective-permute-start(bf16[288,4096]{1,0:T(8,128)(2,1)S(1)} %bitcast.108), channel_id=1, source_target_pairs={{0,32},{32,0},{1,33},{33,1},{2,34},{34,2},{3,35},{35,3},{4,36},{36... | collective-permute-start | bytes 7077896 | tf_op jit(solution)/shard_map/ppermute | solution.py:20
  92.4 31.8 %collective-permute-start.1 = (bf16[288,4096]{1,0:T(8,128)(2,1)}, bf16[288,4096]{1,0:T(8,128)(2,1)}, u32[]{:S(2)}, u32[]{:S(2)}) collective-permute-start(bf16[288,4096]{1,0:T(8,128)(2,1)} %bitcast.9.policy_mine_ref), channel_id=1, source_target_pairs={{0,32},{32,0},{1,33},{33,1},{2,34},{34,2},{3,35},{35,3},{4,36},{36... | collective-permute-start | bytes 7077896 | tf_op jit(solution)/shard_map/ppermute | solution.py:20
  95.0 8.5 %all-to-all-start.4 = ((f32[4,2,144]{2,1,0:T(2,128)}), f32[4,2,144]{2,1,0:T(2,128)S(1)}, u32[]{:S(2)}, u32[]{:S(2)}) async-start(f32[4,2,144]{2,1,0:T(2,128)} %broadcast_in_dim.23), calls=%async_computation.4 | async-start | bytes 16384 | tf_op jit(solution)/shard_map/all_to_all | solution.py:16
  103.5 17.0 %all-to-all-start.3 = ((bf16[4,3,144,256]{3,2,1,0:T(8,128)(2,1)}), bf16[4,3,144,256]{3,2,1,0:T(8,128)(2,1)S(1)}, u32[]{:S(2)}, u32[]{:S(2)}) async-start(bf16[4,3,144,256]{3,2,1,0:T(8,128)(2,1)} %copy.55), calls=%async_computation.3 | async-start | bytes 1769472 | tf_op jit(solution)/shard_map/all_to_all | solution.py:187
  120.7 3.5 %collective-permute-start.2 = (bf16[2,288,256]{2,1,0:T(8,128)(2,1)S(1)}, bf16[2,288,256]{2,1,0:T(8,128)(2,1)S(1)}, u32[]{:S(2)}, u32[]{:S(2)}) collective-permute-start(bf16[2,288,256]{2,1,0:T(8,128)(2,1)S(1)} %pad_maximum_fusion.7.targets_ref), channel_id=1, source_target_pairs={{0,32},{32,0},{1,33},{33,1},{2,34},{34,2},{3,35},{35,3},{4,36},{36... | collective-permute-start | bytes 884744 | tf_op jit(solution)/shard_map/ppermute | solution.py:20
  131.2 18.6 %copy-start.16 = (s32[128,2]{0,1:T(2,128)S(1)}, s32[128,2]{0,1:T(2,128)}, u32[]{:S(2)}) copy-start(s32[128,2]{0,1:T(2,128)} %param.21) | copy-start | bytes 3076
  140.8 23.1 %all-to-all-start.5 = ((f32[16,5,256]{2,1,0:T(8,128)}), f32[16,5,256]{2,1,0:T(8,128)S(1)}, u32[]{:S(2)}, u32[]{:S(2)}) async-start(f32[16,5,256]{2,1,0:T(8,128)} %get-tuple-element.31), calls=%async_computation.5 | async-start | bytes 262144 | tf_op jit(solution)/shard_map/all_to_all | solution.py:205
  149.9 29.2 %collective-permute-start.4 = (bf16[2,4,256,256]{3,2,1,0:T(8,128)(2,1)}, bf16[2,4,256,256]{3,2,1,0:T(8,128)(2,1)S(1)}, u32[]{:S(2)}, u32[]{:S(2)}) collective-permute-start(bf16[2,4,256,256]{3,2,1,0:T(8,128)(2,1)} %get-tuple-element.32), channel_id=1, source_target_pairs={{0,32},{32,0},{1,33},{33,1},{2,34},{34,2},{3,35},{35,3},{4,36},{36... | collective-permute-start | bytes 3145736 | tf_op jit(solution)/shard_map/ppermute | solution.py:20
  152.0 27.0 %collective-permute-start.5 = (f32[2,288,256]{2,1,0:T(8,128)}, f32[2,288,256]{2,1,0:T(8,128)S(1)}, u32[]{:S(2)}, u32[]{:S(2)}) collective-permute-start(f32[2,288,256]{2,1,0:T(8,128)} %get-tuple-element.33), channel_id=1, source_target_pairs={{0,32},{32,0},{1,33},{33,1},{2,34},{34,2},{3,35},{35,3},{4,36},{36... | collective-permute-start | bytes 1769480 | tf_op jit(solution)/shard_map/ppermute | solution.py:20
  164.3 3.1 %collective-permute-start.3 = (f32[776]{0:T(1024)S(1)}, f32[776]{0:T(1024)S(1)}, u32[]{:S(2)}, u32[]{:S(2)}) collective-permute-start(f32[776]{0:T(1024)S(1)} %pad_maximum_fusion.9), channel_id=1, source_target_pairs={{0,32},{32,0},{1,33},{33,1},{2,34},{34,2},{3,35},{35,3},{4,36},{36... | collective-permute-start | bytes 9320 | tf_op jit(solution)/shard_map/ppermute | solution.py:20
  167.4 13.4 %copy-start.2 = (bf16[2,288,256]{2,1,0:T(8,128)(2,1)S(1)}, bf16[2,288,256]{2,1,0:T(8,128)(2,1)}, u32[]{:S(2)}) copy-start(bf16[2,288,256]{2,1,0:T(8,128)(2,1)} %copy-done.1) | copy-start | bytes 884740
  167.4 13.4 %copy-start.3 = (f32[2,288,256]{2,1,0:T(8,128)S(1)}, f32[2,288,256]{2,1,0:T(8,128)}, u32[]{:S(2)}) copy-start(f32[2,288,256]{2,1,0:T(8,128)} %get-tuple-element.33) | copy-start | bytes 1769476
  168.0 11.0 %all-to-all-start.6 = ((f32[16,2,8]{2,1,0:T(2,128)}), f32[16,2,8]{2,1,0:T(2,128)S(1)}, u32[]{:S(2)}, u32[]{:S(2)}) async-start(f32[16,2,8]{2,1,0:T(2,128)} %broadcast_in_dim.24), calls=%async_computation.6 | async-start | bytes 32768 | tf_op jit(solution)/shard_map/all_to_all | solution.py:16
  185.8 21.6 %all-to-all-start.8 = ((bf16[16,144,256]{2,1,0:T(8,128)(2,1)}), bf16[16,144,256]{2,1,0:T(8,128)(2,1)S(1)}, u32[]{:S(2)}, u32[]{:S(2)}) async-start(bf16[16,144,256]{2,1,0:T(8,128)(2,1)} %bitcast.56), calls=%async_computation.8 | async-start | bytes 2359296 | tf_op jit(solution)/shard_map/all_to_all | solution.py:272
  207.4 20.7 %all-to-all-start.7 = ((bf16[16,144,256]{2,1,0:T(8,128)(2,1)}), bf16[16,144,256]{2,1,0:T(8,128)(2,1)S(1)}, u32[]{:S(2)}, u32[]{:S(2)}) async-start(bf16[16,144,256]{2,1,0:T(8,128)(2,1)} %bitcast.47), calls=%async_computation.7 | async-start | bytes 2359296 | tf_op jit(solution)/shard_map/all_to_all | solution.py:272
  213.5 18.8 %collective-permute-start.6 = (f32[144,256]{1,0:T(8,128)S(1)}, f32[144,256]{1,0:T(8,128)S(1)}, u32[]{:S(2)}, u32[]{:S(2)}) collective-permute-start(f32[144,256]{1,0:T(8,128)S(1)} %convert_reduce_fusion), channel_id=1, source_target_pairs={{0,256},{256,0},{1,257},{257,1},{2,258},{258,2},{3,259},{259,3},{4... | collective-permute-start | bytes 442376 | tf_op jit(solution)/shard_map/ppermute | solution.py:20
  (13 other events, 43.1 us)
Sparse Core Ops, SparseCore 0:
  23.5 106.8 all-gather.1

commit v5 on v4

--- a/solution.py
+++ b/solution.py
@@ -98,8 +98,8 @@
                 terms = (hidden * hidden, hidden * (gain * target))
                 for i, term in enumerate(terms):
                     totals[2 * model + i] += jnp.sum(term, axis=0, keepdims=True)
-        totals.append(valid_ref[...])
-        for i in range(5):
+        totals[1], totals[3] = totals[1] * valid_ref[...], totals[3] * valid_ref[...]
+        for i in range(4):
             stats_ref[:, i : i + 1, :] = jnp.broadcast_to(
                 totals[i][None], (2 * NZ, 1, tokens)
             )
@@ -132,10 +132,10 @@
             whole(half_rows, 4),
             whole(1, tokens),
         ],
-        out_specs=[whole(*block), whole(2 * NZ, 5, tokens), whole(*columns), whole(*columns)],
+        out_specs=[whole(*block), whole(2 * NZ, 4, tokens), whole(*columns), whole(*columns)],
         out_shape=[
             jax.ShapeDtypeStruct(block, jnp.float32),
-            jax.ShapeDtypeStruct((2 * NZ, 5, tokens), jnp.float32),
+            jax.ShapeDtypeStruct((2 * NZ, 4, tokens), jnp.float32),
             jax.ShapeDtypeStruct(columns, jnp.bfloat16),
             jax.ShapeDtypeStruct(columns, jnp.bfloat16),
         ],
@@ -202,17 +202,17 @@
     policy_hidden, stats, columns, other_columns = forward(
         core, contexts, policy_rows, frozen_rows, streams, gains, valid
     )
-    stats = lax.all_to_all(stats, ("zh", "zl"), 0, 0).reshape(2, NZ, 5, tokens)
-    valid = stats[:, 0, 4]
-    stats = jnp.sum(stats[:, :, :4], axis=1)
+    stats = lax.all_to_all(stats, ("zh", "zl"), 0, 0).reshape(2, NZ, 4, tokens)
+    stats = jnp.sum(stats, axis=1)
     other_hidden = swapped(policy_hidden, "c")
     other_columns = swapped(other_columns, "c")
 
     scales = lax.rsqrt(stats[:, 0::2] / D + epsilon)
     gap_of_token = scales[:, 0] * stats[:, 1] - scales[:, 1] * stats[:, 3]
-    own_gaps = jnp.sum((gap_of_token * valid).reshape(2 * seqs, seq_len), axis=1)
-    scalars = jnp.stack([scales[:, 0], stats[:, 1], valid], axis=1)
+    own_gaps = jnp.sum(gap_of_token.reshape(2 * seqs, seq_len), axis=1)
+    scalars = jnp.stack([scales[:, 0], stats[:, 1]], axis=1)
     scalars = lax.dynamic_index_in_dim(scalars, z_hi, 0, keepdims=False)
+    scalars = jnp.concatenate([scalars, valid])
     told = jnp.concatenate([own_gaps, scalars.reshape(-1)])
     other_told = swapped(told, "c")
     other_gaps, other_told = other_told[: 2 * seqs], other_told[2 * seqs :].reshape(3, tokens)
@@ -271,7 +271,7 @@
         grad = grad_of(z).astype(jnp.bfloat16).reshape(NX * NY, rows, 256)
         grad = lax.all_to_all(grad, ("x", "y"), 0, 0)
         sums.append(jnp.sum(grad.astype(jnp.float32), axis=0))
-    weight_grad = sums[1] + swapped(sums[0], "zh")
+    weight_grad = sums[1] + swapped(sums[0].astype(jnp.bfloat16), "zh").astype(jnp.float32)
     return (weight_grad, margins, loss)
 
 

time: 244 us -> 238 us (0.975); the launches traced: 240 us -> 237 us
    ppermute x7, waiting for transfers between devices: 5.2 us -> 2.32 us  [swapped(): return lax.ppermute(value, axis, [(0, 1), (1, 0)])]
    unnamed x47 -> x49, local copies, waits for them, and re-layouts: 5.7 us -> 5.72 us
where the time goes in v5:
time: 238 us; the launch traced here: 237 us
  waiting for transfers between devices  112 us (47%)
  starting transfers between devices  56.9 us (24%)
  local copies, waits for them, and re-layouts  17.3 us (7%)
  between operations  14.7 us (6%)
  blocking collectives  13.7 us (6%)
  Pallas kernels  9.91 us (4%)
  other arithmetic  8.67 us (4%)
  matrix products  3.68 us (2%)
    all_to_all x4, waiting for transfers between devices, spread(): lax.all_to_all(jnp.broadcast_to(value[None], (count,) + value.shape), axe...  58.8 us
    all_to_all x2, waiting for transfers between devices, shards(): grad = lax.all_to_all(grad, ('x', 'y'), 0, 0)  23.2 us
    all_to_all x4, starting transfers between devices, spread(): lax.all_to_all(jnp.broadcast_to(value[None], (count,) + value.shape), axe...  16.9 us
    ppermute x7, starting transfers between devices, swapped(): return lax.ppermute(value, axis, [(0, 1), (1, 0)])  15.7 us
    all_to_all x1, blocking collectives, shards(): contexts = lax.all_to_all(contexts, 'y', 0, 0)  13.7 us
    all_to_all x1, waiting for transfers between devices, shards(): streams = lax.all_to_all(streams, 'y', 0, 0)  12.2 us
    all_to_all x2, starting transfers between devices, shards(): grad = lax.all_to_all(grad, ('x', 'y'), 0, 0)  11.7 us
    pallas_call x1, Pallas kernels, forward(): pl.pallas_call(forward_step, grid=(NZ // 2,), in_specs=[pl.BlockSpec(memo...  9.91 us
  transfers between devices with their start and end apart: 16, of which 11 were waited for; matrix products, arithmetic and copies ran while one was open for 8% of the time, Pallas kernels for 0%

profile of v5, /device:TPU:6, one launch (start us, length us, event | category | flops | bytes accessed | tf_op | source)
XLA Modules:
  0.0 236.6 jit_solution(10446843673764856275)
XLA Ops:
  8.3 13.7 %all_to_all.45 = bf16[4,2,256,128]{3,2,1,0:T(8,128)(2,1)S(1)} all-to-all(bf16[4,2,256,128]{3,2,1,0:T(8,128)(2,1)S(1)} %pad_maximum_fusion.4), channel_id=1, replica_groups=mesh['zh'=2,'x'=4,'c'=2,'y'=4,'zl'=8] {'y'}, dimensions={0} | all-to-all | bytes 1048576 | tf_op jit(solution)/shard_map/all_to_all | solution.py:174
  26.5 3.6 %all-to-all-start.1 = ((bf16[4,72,4096]{2,1,0:T(8,128)(2,1)}), bf16[4,72,4096]{2,1,0:T(8,128)(2,1)S(1)}, u32[]{:S(2)}, u32[]{:S(2)}) async-start(bf16[4,72,4096]{2,1,0:T(8,128)(2,1)} %broadcast_in_dim.20), calls=%async_computation.1 | async-start | bytes 4718592 | tf_op jit(solution)/shard_map/all_to_all | solution.py:16
  30.9 27.4 %all-to-all-done.1 = bf16[4,72,4096]{2,1,0:T(8,128)(2,1)S(1)} async-done(((bf16[4,72,4096]{2,1,0:T(8,128)(2,1)}), bf16[4,72,4096]{2,1,0:T(8,128)(2,1)S(1)}, u32[]{:S(2)}, u32[]{:S(2)}) %all-to-all-start.1) | async-done | bytes 2359328 | tf_op jit(solution)/shard_map/all_to_all | solution.py:16
  60.3 4.7 %all-to-all-start.2 = ((bf16[4,72,4096]{2,1,0:T(8,128)(2,1)}), bf16[4,72,4096]{2,1,0:T(8,128)(2,1)}, u32[]{:S(2)}, u32[]{:S(2)}) async-start(bf16[4,72,4096]{2,1,0:T(8,128)(2,1)} %broadcast_in_dim.22), calls=%async_computation.2 | async-start | bytes 4718592 | tf_op jit(solution)/shard_map/all_to_all | solution.py:16
  65.0 2.1 collective-permute-start
  67.1 25.3 %all-to-all-done.2 = bf16[4,72,4096]{2,1,0:T(8,128)(2,1)} async-done(((bf16[4,72,4096]{2,1,0:T(8,128)(2,1)}), bf16[4,72,4096]{2,1,0:T(8,128)(2,1)}, u32[]{:S(2)}, u32[]{:S(2)}) %all-to-all-start.2) | async-done | bytes 2359328 | tf_op jit(solution)/shard_map/all_to_all | solution.py:16
  94.9 3.2 %all-to-all-start.4 = ((f32[4,2,144]{2,1,0:T(2,128)}), f32[4,2,144]{2,1,0:T(2,128)S(1)}, u32[]{:S(2)}, u32[]{:S(2)}) async-start(f32[4,2,144]{2,1,0:T(2,128)} %broadcast_in_dim.23), calls=%async_computation.4 | async-start | bytes 16384 | tf_op jit(solution)/shard_map/all_to_all | solution.py:16
  100.6 2.9 %all-to-all-done.4 = f32[4,2,144]{2,1,0:T(2,128)S(1)} async-done(((f32[4,2,144]{2,1,0:T(2,128)}), f32[4,2,144]{2,1,0:T(2,128)S(1)}, u32[]{:S(2)}, u32[]{:S(2)}) %all-to-all-start.4) | async-done | bytes 4640 | tf_op jit(solution)/shard_map/all_to_all | solution.py:16
  103.5 3.5 %all-to-all-start.3 = ((bf16[4,3,144,256]{3,2,1,0:T(8,128)(2,1)}), bf16[4,3,144,256]{3,2,1,0:T(8,128)(2,1)S(1)}, u32[]{:S(2)}, u32[]{:S(2)}) async-start(bf16[4,3,144,256]{3,2,1,0:T(8,128)(2,1)} %copy.64), calls=%async_computation.3 | async-start | bytes 1769472 | tf_op jit(solution)/shard_map/all_to_all | solution.py:187
  108.3 12.2 %all-to-all-done.3 = bf16[4,3,144,256]{3,2,1,0:T(8,128)(2,1)S(1)} async-done(((bf16[4,3,144,256]{3,2,1,0:T(8,128)(2,1)}), bf16[4,3,144,256]{3,2,1,0:T(8,128)(2,1)S(1)}, u32[]{:S(2)}, u32[]{:S(2)}) %all-to-all-start.3) | async-done | bytes 884768 | tf_op jit(solution)/shard_map/all_to_all | solution.py:187
  124.1 6.3 %all-gather.2.cloned.1.call-done.context_ref = bf16[512,4096]{1,0:T(8,128)(2,1)} async-done(((bf16[512,512]{1,0:T(8,128)(2,1)}), bf16[512,4096]{1,0:T(8,128)(2,1)}) %all-gather.2.cloned.1.call-update) | async-done | bytes 4194320 | tf_op jit(solution)/shard_map/all_gather | solution.py:176
  131.2 9.9 %shard_map.130 = (f32[2,288,256]{2,1,0:T(8,128)}, f32[16,4,256]{2,1,0:T(4,128)}, bf16[2,4,256,256]{3,2,1,0:T(8,128)(2,1)}, bf16[2,4,256,256]{3,2,1,0:T(8,128)(2,1)}) custom-call(s32[1]{0:T(128)} %bitcast.2.core_ref, bf16[512,4096]{1,0:T(8,128)(2,1)} %all-gather.2.cloned.1.call-done.context_ref, bf16[288,4096]{1,0:T(8,128)(2,1)} %bitcast.9.policy_mine_ref, ...), custom_call_target="tpu_custom_call" | custom-call | flops 2415919104 | bytes 15728640 | tf_op jit(solution)/shard_map/pallas_call | solution.py:119
  141.1 9.0 %all-to-all-start.5 = ((f32[16,4,256]{2,1,0:T(4,128)}), f32[16,4,256]{2,1,0:T(4,128)S(1)}, u32[]{:S(2)}, u32[]{:S(2)}) async-start(f32[16,4,256]{2,1,0:T(4,128)} %get-tuple-element.31), calls=%async_computation.5 | async-start | bytes 131072 | tf_op jit(solution)/shard_map/all_to_all | solution.py:205
  150.2 2.1 collective-permute-start.4
  152.3 2.2 collective-permute-start.5
  154.6 9.0 %all-to-all-done.5 = f32[16,4,256]{2,1,0:T(4,128)S(1)} async-done(((f32[16,4,256]{2,1,0:T(4,128)}), f32[16,4,256]{2,1,0:T(4,128)S(1)}, u32[]{:S(2)}, u32[]{:S(2)}) %all-to-all-start.5) | async-done | bytes 65568 | tf_op jit(solution)/shard_map/all_to_all | solution.py:205
  167.6 5.4 %all-to-all-start.6 = ((f32[16,2,8]{2,1,0:T(2,128)}), f32[16,2,8]{2,1,0:T(2,128)S(1)}, u32[]{:S(2)}, u32[]{:S(2)}) async-start(f32[16,2,8]{2,1,0:T(2,128)} %broadcast_in_dim.24), calls=%async_computation.6 | async-start | bytes 32768 | tf_op jit(solution)/shard_map/all_to_all | solution.py:16
  173.0 2.3 constant_dynamic-update-slice_fusion.1
  175.5 3.2 %all-to-all-done.6 = f32[16,2,8]{2,1,0:T(2,128)S(1)} async-done(((f32[16,2,8]{2,1,0:T(2,128)}), f32[16,2,8]{2,1,0:T(2,128)S(1)}, u32[]{:S(2)}, u32[]{:S(2)}) %all-to-all-start.6) | async-done | bytes 1056 | tf_op jit(solution)/shard_map/all_to_all | solution.py:16
  185.4 5.8 %all-to-all-start.8 = ((bf16[16,144,256]{2,1,0:T(8,128)(2,1)}), bf16[16,144,256]{2,1,0:T(8,128)(2,1)S(1)}, u32[]{:S(2)}, u32[]{:S(2)}) async-start(bf16[16,144,256]{2,1,0:T(8,128)(2,1)} %bitcast.57), calls=%async_computation.8 | async-start | bytes 2359296 | tf_op jit(solution)/shard_map/all_to_all | solution.py:272
  194.9 12.2 %all-to-all-done.8 = bf16[16,144,256]{2,1,0:T(8,128)(2,1)S(1)} async-done(((bf16[16,144,256]{2,1,0:T(8,128)(2,1)}), bf16[16,144,256]{2,1,0:T(8,128)(2,1)S(1)}, u32[]{:S(2)}, u32[]{:S(2)}) %all-to-all-start.8) | async-done | bytes 1179680 | tf_op jit(solution)/shard_map/all_to_all | solution.py:272
  207.1 5.9 %all-to-all-start.7 = ((bf16[16,144,256]{2,1,0:T(8,128)(2,1)}), bf16[16,144,256]{2,1,0:T(8,128)(2,1)S(1)}, u32[]{:S(2)}, u32[]{:S(2)}) async-start(bf16[16,144,256]{2,1,0:T(8,128)(2,1)} %bitcast.48), calls=%async_computation.7 | async-start | bytes 2359296 | tf_op jit(solution)/shard_map/all_to_all | solution.py:272
  213.1 3.6 %collective-permute-start.6 = (bf16[144,256]{1,0:T(8,128)(2,1)S(1)}, bf16[144,256]{1,0:T(8,128)(2,1)S(1)}, u32[]{:S(2)}, u32[]{:S(2)}) collective-permute-start(bf16[144,256]{1,0:T(8,128)(2,1)S(1)} %reduce_sum.81), channel_id=1, source_target_pairs={{0,256},{256,0},{1,257},{257,1},{2,258},{258,2},{3,259},{259,3},{4... | collective-permute-start | bytes 221192 | tf_op jit(solution)/shard_map/ppermute | solution.py:20
  216.7 11.0 %all-to-all-done.7 = bf16[16,144,256]{2,1,0:T(8,128)(2,1)S(1)} async-done(((bf16[16,144,256]{2,1,0:T(8,128)(2,1)}), bf16[16,144,256]{2,1,0:T(8,128)(2,1)S(1)}, u32[]{:S(2)}, u32[]{:S(2)}) %all-to-all-start.7) | async-done | bytes 1179680 | tf_op jit(solution)/shard_map/all_to_all | solution.py:272
  (146 shorter events, 35.4 us)
Async XLA Ops:
  7.2 123.2 %all-gather.2.cloned.1.call-start = ((), (), s32[]{:S(2)}) async-start(), calls=%async_computation.9 | async-start | bytes 4718592 | tf_op jit(solution)/shard_map/all_gather | solution.py:176
  26.5 31.8 %all-to-all-start.1 = ((bf16[4,72,4096]{2,1,0:T(8,128)(2,1)}), bf16[4,72,4096]{2,1,0:T(8,128)(2,1)S(1)}, u32[]{:S(2)}, u32[]{:S(2)}) async-start(bf16[4,72,4096]{2,1,0:T(8,128)(2,1)} %broadcast_in_dim.20), calls=%async_computation.1 | async-start | bytes 4718592 | tf_op jit(solution)/shard_map/all_to_all | solution.py:16
  60.3 34.0 %copy-start.18 = (f32[144]{0:T(256)S(1)}, f32[144]{0:T(256)}, u32[]{:S(2)}) copy-start(f32[144]{0:T(256)} %param.17) | copy-start | bytes 1732
  60.3 34.0 %copy-start.19 = (f32[144]{0:T(256)S(1)}, f32[144]{0:T(256)}, u32[]{:S(2)}) copy-start(f32[144]{0:T(256)} %param.16) | copy-start | bytes 1732
  60.3 37.9 %copy-start.9 = (bf16[144,1024]{1,0:T(8,128)(2,1)S(1)}, bf16[144,1024]{1,0:T(8,128)(2,1)}, u32[]{:S(2)}) copy-start(bf16[144,1024]{1,0:T(8,128)(2,1)} %param.13) | copy-start | bytes 884740
  60.3 38.1 %copy-start.10 = (bf16[144,1024]{1,0:T(8,128)(2,1)S(1)}, bf16[144,1024]{1,0:T(8,128)(2,1)}, u32[]{:S(2)}) copy-start(bf16[144,1024]{1,0:T(8,128)(2,1)} %param.14) | copy-start | bytes 884740
  60.3 32.1 %all-to-all-start.2 = ((bf16[4,72,4096]{2,1,0:T(8,128)(2,1)}), bf16[4,72,4096]{2,1,0:T(8,128)(2,1)}, u32[]{:S(2)}, u32[]{:S(2)}) async-start(bf16[4,72,4096]{2,1,0:T(8,128)(2,1)} %broadcast_in_dim.22), calls=%async_computation.2 | async-start | bytes 4718592 | tf_op jit(solution)/shard_map/all_to_all | solution.py:16
  65.0 33.6 %copy-start.11 = (bf16[144,1024]{1,0:T(8,128)(2,1)S(1)}, bf16[144,1024]{1,0:T(8,128)(2,1)}, u32[]{:S(2)}) copy-start(bf16[144,1024]{1,0:T(8,128)(2,1)} %param.15) | copy-start | bytes 884740
  65.0 59.1 %collective-permute-start = (bf16[288,4096]{1,0:T(8,128)(2,1)S(1)}, bf16[288,4096]{1,0:T(8,128)(2,1)}, u32[]{:S(2)}, u32[]{:S(2)}) collective-permute-start(bf16[288,4096]{1,0:T(8,128)(2,1)S(1)} %bitcast.112), channel_id=1, source_target_pairs={{0,32},{32,0},{1,33},{33,1},{2,34},{34,2},{3,35},{35,3},{4,36},{36... | collective-permute-start | bytes 7077896 | tf_op jit(solution)/shard_map/ppermute | solution.py:20
  92.4 31.8 %collective-permute-start.1 = (bf16[288,4096]{1,0:T(8,128)(2,1)}, bf16[288,4096]{1,0:T(8,128)(2,1)}, u32[]{:S(2)}, u32[]{:S(2)}) collective-permute-start(bf16[288,4096]{1,0:T(8,128)(2,1)} %bitcast.9.policy_mine_ref), channel_id=1, source_target_pairs={{0,32},{32,0},{1,33},{33,1},{2,34},{34,2},{3,35},{35,3},{4,36},{36... | collective-permute-start | bytes 7077896 | tf_op jit(solution)/shard_map/ppermute | solution.py:20
  94.9 8.5 %all-to-all-start.4 = ((f32[4,2,144]{2,1,0:T(2,128)}), f32[4,2,144]{2,1,0:T(2,128)S(1)}, u32[]{:S(2)}, u32[]{:S(2)}) async-start(f32[4,2,144]{2,1,0:T(2,128)} %broadcast_in_dim.23), calls=%async_computation.4 | async-start | bytes 16384 | tf_op jit(solution)/shard_map/all_to_all | solution.py:16
  103.5 17.0 %all-to-all-start.3 = ((bf16[4,3,144,256]{3,2,1,0:T(8,128)(2,1)}), bf16[4,3,144,256]{3,2,1,0:T(8,128)(2,1)S(1)}, u32[]{:S(2)}, u32[]{:S(2)}) async-start(bf16[4,3,144,256]{3,2,1,0:T(8,128)(2,1)} %copy.64), calls=%async_computation.3 | async-start | bytes 1769472 | tf_op jit(solution)/shard_map/all_to_all | solution.py:187
  120.7 3.5 %collective-permute-start.2 = (bf16[2,288,256]{2,1,0:T(8,128)(2,1)S(1)}, bf16[2,288,256]{2,1,0:T(8,128)(2,1)S(1)}, u32[]{:S(2)}, u32[]{:S(2)}) collective-permute-start(bf16[2,288,256]{2,1,0:T(8,128)(2,1)S(1)} %pad_maximum_fusion.7.targets_ref), channel_id=1, source_target_pairs={{0,32},{32,0},{1,33},{33,1},{2,34},{34,2},{3,35},{35,3},{4,36},{36... | collective-permute-start | bytes 884744 | tf_op jit(solution)/shard_map/ppermute | solution.py:20
  131.2 19.0 %copy-start.17 = (s32[128,2]{0,1:T(2,128)S(1)}, s32[128,2]{0,1:T(2,128)}, u32[]{:S(2)}) copy-start(s32[128,2]{0,1:T(2,128)} %param.21) | copy-start | bytes 3076
  131.2 32.4 %copy-start.16 = (f32[1,256]{1,0:T(1,128)S(1)}, f32[1,256]{1,0:T(1,128)}, u32[]{:S(2)}) copy-start(f32[1,256]{1,0:T(1,128)} %reshape.280.valid_ref) | copy-start | bytes 3076
  141.1 22.4 %all-to-all-start.5 = ((f32[16,4,256]{2,1,0:T(4,128)}), f32[16,4,256]{2,1,0:T(4,128)S(1)}, u32[]{:S(2)}, u32[]{:S(2)}) async-start(f32[16,4,256]{2,1,0:T(4,128)} %get-tuple-element.31), calls=%async_computation.5 | async-start | bytes 131072 | tf_op jit(solution)/shard_map/all_to_all | solution.py:205
  150.2 28.4 %collective-permute-start.4 = (bf16[2,4,256,256]{3,2,1,0:T(8,128)(2,1)}, bf16[2,4,256,256]{3,2,1,0:T(8,128)(2,1)S(1)}, u32[]{:S(2)}, u32[]{:S(2)}) collective-permute-start(bf16[2,4,256,256]{3,2,1,0:T(8,128)(2,1)} %get-tuple-element.32), channel_id=1, source_target_pairs={{0,32},{32,0},{1,33},{33,1},{2,34},{34,2},{3,35},{35,3},{4,36},{36... | collective-permute-start | bytes 3145736 | tf_op jit(solution)/shard_map/ppermute | solution.py:20
  152.3 26.3 %collective-permute-start.5 = (f32[2,288,256]{2,1,0:T(8,128)}, f32[2,288,256]{2,1,0:T(8,128)S(1)}, u32[]{:S(2)}, u32[]{:S(2)}) collective-permute-start(f32[2,288,256]{2,1,0:T(8,128)} %get-tuple-element.33), channel_id=1, source_target_pairs={{0,32},{32,0},{1,33},{33,1},{2,34},{34,2},{3,35},{35,3},{4,36},{36... | collective-permute-start | bytes 1769480 | tf_op jit(solution)/shard_map/ppermute | solution.py:20
  163.9 3.0 %collective-permute-start.3 = (f32[776]{0:T(1024)S(1)}, f32[776]{0:T(1024)S(1)}, u32[]{:S(2)}, u32[]{:S(2)}) collective-permute-start(f32[776]{0:T(1024)S(1)} %pad_maximum_fusion.10), channel_id=1, source_target_pairs={{0,32},{32,0},{1,33},{33,1},{2,34},{34,2},{3,35},{35,3},{4,36},{36... | collective-permute-start | bytes 9320 | tf_op jit(solution)/shard_map/ppermute | solution.py:20
  167.0 13.4 %copy-start.2 = (bf16[2,288,256]{2,1,0:T(8,128)(2,1)S(1)}, bf16[2,288,256]{2,1,0:T(8,128)(2,1)}, u32[]{:S(2)}) copy-start(bf16[2,288,256]{2,1,0:T(8,128)(2,1)} %copy-done.1) | copy-start | bytes 884740
  167.6 11.0 %all-to-all-start.6 = ((f32[16,2,8]{2,1,0:T(2,128)}), f32[16,2,8]{2,1,0:T(2,128)S(1)}, u32[]{:S(2)}, u32[]{:S(2)}) async-start(f32[16,2,8]{2,1,0:T(2,128)} %broadcast_in_dim.24), calls=%async_computation.6 | async-start | bytes 32768 | tf_op jit(solution)/shard_map/all_to_all | solution.py:16
  185.4 21.6 %all-to-all-start.8 = ((bf16[16,144,256]{2,1,0:T(8,128)(2,1)}), bf16[16,144,256]{2,1,0:T(8,128)(2,1)S(1)}, u32[]{:S(2)}, u32[]{:S(2)}) async-start(bf16[16,144,256]{2,1,0:T(8,128)(2,1)} %bitcast.57), calls=%async_computation.8 | async-start | bytes 2359296 | tf_op jit(solution)/shard_map/all_to_all | solution.py:272
  207.1 20.7 %all-to-all-start.7 = ((bf16[16,144,256]{2,1,0:T(8,128)(2,1)}), bf16[16,144,256]{2,1,0:T(8,128)(2,1)S(1)}, u32[]{:S(2)}, u32[]{:S(2)}) async-start(bf16[16,144,256]{2,1,0:T(8,128)(2,1)} %bitcast.48), calls=%async_computation.7 | async-start | bytes 2359296 | tf_op jit(solution)/shard_map/all_to_all | solution.py:272
  213.1 15.9 %collective-permute-start.6 = (bf16[144,256]{1,0:T(8,128)(2,1)S(1)}, bf16[144,256]{1,0:T(8,128)(2,1)S(1)}, u32[]{:S(2)}, u32[]{:S(2)}) collective-permute-start(bf16[144,256]{1,0:T(8,128)(2,1)S(1)} %reduce_sum.81), channel_id=1, source_target_pairs={{0,256},{256,0},{1,257},{257,1},{2,258},{258,2},{3,259},{259,3},{4... | collective-permute-start | bytes 221192 | tf_op jit(solution)/shard_map/ppermute | solution.py:20
  (14 other events, 56.4 us)
Sparse Core Ops, SparseCore 0:
  23.5 106.8 all-gather.1

commit v6 on v5

--- a/solution.py
+++ b/solution.py
@@ -166,7 +166,7 @@
     seq_len = tokens_here // valid_lengths.shape[0]
     seqs = valid_lengths.shape[0] // NY
     tokens = tokens_here // NY
-    z_hi, core, y = lax.axis_index("zh"), lax.axis_index("c"), lax.axis_index("y")
+    z_hi, x, core, y = (lax.axis_index(name) for name in ("zh", "x", "c", "y"))
 
     contexts = jnp.stack(
         [policy_context.reshape(NY, tokens, 128), frozen_context.reshape(NY, tokens, 128)], axis=1
@@ -214,16 +214,13 @@
     scalars = lax.dynamic_index_in_dim(scalars, z_hi, 0, keepdims=False)
     scalars = jnp.concatenate([scalars, valid])
     told = jnp.concatenate([own_gaps, scalars.reshape(-1)])
-    other_told = swapped(told, "c")
-    other_gaps, other_told = other_told[: 2 * seqs], other_told[2 * seqs :].reshape(3, tokens)
-    chip_gaps = jnp.where(
-        core == 0, jnp.stack([own_gaps, other_gaps]), jnp.stack([other_gaps, own_gaps])
-    )
-    gaps = spread(chip_gaps, ("x", "y"), NX * NY)
-    gaps, other_columns, other_hidden = lax.optimization_barrier(
-        (gaps, other_columns, other_hidden)
-    )
-    gaps = gaps.reshape(NX, NY, 2, 2, seqs).transpose(3, 0, 2, 1, 4).reshape(-1)
+    told = spread(told, ("x", "c", "y"), NX * 2 * NY)
+    told, other_columns, other_hidden = lax.optimization_barrier(
+        (told, other_columns, other_hidden)
+    )
+    gaps = told[:, : 2 * seqs].reshape(NX, 2, NY, 2, seqs).transpose(3, 0, 1, 2, 4).reshape(-1)
+    other_scalars = lax.dynamic_index_in_dim(told, (x * 2 + 1 - core) * NY + y, 0, keepdims=False)
+    other_scalars = other_scalars[2 * seqs :].reshape(3, tokens)
 
     total_seqs = gaps.shape[0]
     pair_count = pair_rows.shape[0]
@@ -254,7 +251,7 @@
 
     own_grad = hidden_grad_of(core, *scalars, policy_gain, streams[2], policy_hidden)
     other_grad = hidden_grad_of(
-        1 - core, *other_told, policy_gain[::-1], other_targets, other_hidden
+        1 - core, *other_scalars, policy_gain[::-1], other_targets, other_hidden
     )
     hidden_grad = jnp.concatenate([own_grad, other_grad], axis=1)
     columns = jnp.concatenate([columns, other_columns], axis=2)

time: 238 us -> 238 us (level)
    ppermute x7 -> x6, starting transfers between devices: 15.7 us -> 13.9 us  [swapped(): return lax.ppermute(value, axis, [(0, 1), (1, 0)])]
    unnamed x49 -> x50, local copies, waits for them, and re-layouts: 5.72 us -> 5.82 us
  transfers between devices with their start and end apart: 16 -> 15, of which waited for: 11 -> 10; matrix products, arithmetic and copies ran while one was open for 8% -> 8% of each run, Pallas kernels for 0% -> 0%
where the time goes in v6:
time: 238 us; the launch traced here: 237 us
  waiting for transfers between devices  113 us (47%)
  starting transfers between devices  55.4 us (23%)
  local copies, waits for them, and re-layouts  17.6 us (7%)
  between operations  14.7 us (6%)
  blocking collectives  13.7 us (6%)
  Pallas kernels  9.91 us (4%)
  other arithmetic  8.59 us (4%)
  matrix products  3.68 us (2%)
    all_to_all x4, waiting for transfers between devices, spread(): lax.all_to_all(jnp.broadcast_to(value[None], (count,) + value.shape), axe...  58.8 us
    all_to_all x2, waiting for transfers between devices, shards(): grad = lax.all_to_all(grad, ('x', 'y'), 0, 0)  25.6 us
    all_to_all x4, starting transfers between devices, spread(): lax.all_to_all(jnp.broadcast_to(value[None], (count,) + value.shape), axe...  17.1 us
    ppermute x6, starting transfers between devices, swapped(): return lax.ppermute(value, axis, [(0, 1), (1, 0)])  13.9 us
    all_to_all x1, blocking collectives, shards(): contexts = lax.all_to_all(contexts, 'y', 0, 0)  13.7 us
    all_to_all x1, waiting for transfers between devices, shards(): streams = lax.all_to_all(streams, 'y', 0, 0)  12.3 us
    all_to_all x2, starting transfers between devices, shards(): grad = lax.all_to_all(grad, ('x', 'y'), 0, 0)  11.8 us
    pallas_call x1, Pallas kernels, forward(): pl.pallas_call(forward_step, grid=(NZ // 2,), in_specs=[pl.BlockSpec(memo...  9.91 us
  transfers between devices with their start and end apart: 15, of which 10 were waited for; matrix products, arithmetic and copies ran while one was open for 8% of the time, Pallas kernels for 0%

profile of v6, /device:TPU:6, one launch (start us, length us, event | category | flops | bytes accessed | tf_op | source)
XLA Modules:
  0.0 237.1 jit_solution(16768398732992499275)
XLA Ops:
  8.3 13.7 %all_to_all.49 = bf16[4,2,256,128]{3,2,1,0:T(8,128)(2,1)S(1)} all-to-all(bf16[4,2,256,128]{3,2,1,0:T(8,128)(2,1)S(1)} %pad_maximum_fusion.4), channel_id=1, replica_groups=mesh['zh'=2,'x'=4,'c'=2,'y'=4,'zl'=8] {'y'}, dimensions={0} | all-to-all | bytes 1048576 | tf_op jit(solution)/shard_map/all_to_all | solution.py:174
  26.5 3.6 %all-to-all-start.1 = ((bf16[4,72,4096]{2,1,0:T(8,128)(2,1)}), bf16[4,72,4096]{2,1,0:T(8,128)(2,1)S(1)}, u32[]{:S(2)}, u32[]{:S(2)}) async-start(bf16[4,72,4096]{2,1,0:T(8,128)(2,1)} %broadcast_in_dim.20), calls=%async_computation.1 | async-start | bytes 4718592 | tf_op jit(solution)/shard_map/all_to_all | solution.py:16
  30.9 27.4 %all-to-all-done.1 = bf16[4,72,4096]{2,1,0:T(8,128)(2,1)S(1)} async-done(((bf16[4,72,4096]{2,1,0:T(8,128)(2,1)}), bf16[4,72,4096]{2,1,0:T(8,128)(2,1)S(1)}, u32[]{:S(2)}, u32[]{:S(2)}) %all-to-all-start.1) | async-done | bytes 2359328 | tf_op jit(solution)/shard_map/all_to_all | solution.py:16
  60.3 4.7 %all-to-all-start.2 = ((bf16[4,72,4096]{2,1,0:T(8,128)(2,1)}), bf16[4,72,4096]{2,1,0:T(8,128)(2,1)}, u32[]{:S(2)}, u32[]{:S(2)}) async-start(bf16[4,72,4096]{2,1,0:T(8,128)(2,1)} %broadcast_in_dim.22), calls=%async_computation.2 | async-start | bytes 4718592 | tf_op jit(solution)/shard_map/all_to_all | solution.py:16
  65.0 2.1 collective-permute-start
  67.1 25.3 %all-to-all-done.2 = bf16[4,72,4096]{2,1,0:T(8,128)(2,1)} async-done(((bf16[4,72,4096]{2,1,0:T(8,128)(2,1)}), bf16[4,72,4096]{2,1,0:T(8,128)(2,1)}, u32[]{:S(2)}, u32[]{:S(2)}) %all-to-all-start.2) | async-done | bytes 2359328 | tf_op jit(solution)/shard_map/all_to_all | solution.py:16
  94.9 3.2 %all-to-all-start.4 = ((f32[4,2,144]{2,1,0:T(2,128)}), f32[4,2,144]{2,1,0:T(2,128)S(1)}, u32[]{:S(2)}, u32[]{:S(2)}) async-start(f32[4,2,144]{2,1,0:T(2,128)} %broadcast_in_dim.23), calls=%async_computation.4 | async-start | bytes 16384 | tf_op jit(solution)/shard_map/all_to_all | solution.py:16
  100.7 2.8 %all-to-all-done.4 = f32[4,2,144]{2,1,0:T(2,128)S(1)} async-done(((f32[4,2,144]{2,1,0:T(2,128)}), f32[4,2,144]{2,1,0:T(2,128)S(1)}, u32[]{:S(2)}, u32[]{:S(2)}) %all-to-all-start.4) | async-done | bytes 4640 | tf_op jit(solution)/shard_map/all_to_all | solution.py:16
  103.5 3.5 %all-to-all-start.3 = ((bf16[4,3,144,256]{3,2,1,0:T(8,128)(2,1)}), bf16[4,3,144,256]{3,2,1,0:T(8,128)(2,1)S(1)}, u32[]{:S(2)}, u32[]{:S(2)}) async-start(bf16[4,3,144,256]{3,2,1,0:T(8,128)(2,1)} %copy.65), calls=%async_computation.3 | async-start | bytes 1769472 | tf_op jit(solution)/shard_map/all_to_all | solution.py:187
  108.2 12.3 %all-to-all-done.3 = bf16[4,3,144,256]{3,2,1,0:T(8,128)(2,1)S(1)} async-done(((bf16[4,3,144,256]{3,2,1,0:T(8,128)(2,1)}), bf16[4,3,144,256]{3,2,1,0:T(8,128)(2,1)S(1)}, u32[]{:S(2)}, u32[]{:S(2)}) %all-to-all-start.3) | async-done | bytes 884768 | tf_op jit(solution)/shard_map/all_to_all | solution.py:187
  124.1 6.3 %all-gather.2.cloned.1.call-done.context_ref = bf16[512,4096]{1,0:T(8,128)(2,1)} async-done(((bf16[512,512]{1,0:T(8,128)(2,1)}), bf16[512,4096]{1,0:T(8,128)(2,1)}) %all-gather.2.cloned.1.call-update) | async-done | bytes 4194320 | tf_op jit(solution)/shard_map/all_gather | solution.py:176
  131.2 9.9 %shard_map.130 = (f32[2,288,256]{2,1,0:T(8,128)}, f32[16,4,256]{2,1,0:T(4,128)}, bf16[2,4,256,256]{3,2,1,0:T(8,128)(2,1)}, bf16[2,4,256,256]{3,2,1,0:T(8,128)(2,1)}) custom-call(s32[1]{0:T(128)} %bitcast.2.core_ref, bf16[512,4096]{1,0:T(8,128)(2,1)} %all-gather.2.cloned.1.call-done.context_ref, bf16[288,4096]{1,0:T(8,128)(2,1)} %bitcast.9.policy_mine_ref, ...), custom_call_target="tpu_custom_call" | custom-call | flops 2415919104 | bytes 15728640 | tf_op jit(solution)/shard_map/pallas_call | solution.py:119
  141.1 9.0 %all-to-all-start.5 = ((f32[16,4,256]{2,1,0:T(4,128)}), f32[16,4,256]{2,1,0:T(4,128)S(1)}, u32[]{:S(2)}, u32[]{:S(2)}) async-start(f32[16,4,256]{2,1,0:T(4,128)} %get-tuple-element.31), calls=%async_computation.5 | async-start | bytes 131072 | tf_op jit(solution)/shard_map/all_to_all | solution.py:205
  150.2 2.1 collective-permute-start.3
  152.3 2.2 collective-permute-start.4
  154.7 8.9 %all-to-all-done.5 = f32[16,4,256]{2,1,0:T(4,128)S(1)} async-done(((f32[16,4,256]{2,1,0:T(4,128)}), f32[16,4,256]{2,1,0:T(4,128)S(1)}, u32[]{:S(2)}, u32[]{:S(2)}) %all-to-all-start.5) | async-done | bytes 65568 | tf_op jit(solution)/shard_map/all_to_all | solution.py:205
  164.7 5.6 %all-to-all-start.6 = ((f32[32,1,776]{2,1,0:T(1,128)}), f32[32,1,776]{2,1,0:T(1,128)S(1)}, u32[]{:S(2)}, u32[]{:S(2)}) async-start(f32[32,1,776]{2,1,0:T(1,128)} %broadcast_in_dim.24), calls=%async_computation.6 | async-start | bytes 229376 | tf_op jit(solution)/shard_map/all_to_all | solution.py:16
  170.3 2.4 %constant_dynamic-update-slice_fusion.1 = bf16[2,4,512,256]{3,2,1,0:T(8,128)(2,1)} fusion(bf16[2,4,256,256]{3,2,1,0:T(8,128)(2,1)} %get-tuple-element.37), kind=kLoop, calls=%fused_computation.48 | loop fusion | bytes 2097152
  172.7 3.3 %all-to-all-done.6 = f32[32,1,776]{2,1,0:T(1,128)S(1)} async-done(((f32[32,1,776]{2,1,0:T(1,128)}), f32[32,1,776]{2,1,0:T(1,128)S(1)}, u32[]{:S(2)}, u32[]{:S(2)}) %all-to-all-start.6) | async-done | bytes 99360 | tf_op jit(solution)/shard_map/all_to_all | solution.py:16
  182.8 5.8 %all-to-all-start.8 = ((bf16[16,144,256]{2,1,0:T(8,128)(2,1)}), bf16[16,144,256]{2,1,0:T(8,128)(2,1)S(1)}, u32[]{:S(2)}, u32[]{:S(2)}) async-start(bf16[16,144,256]{2,1,0:T(8,128)(2,1)} %bitcast.58), calls=%async_computation.8 | async-start | bytes 2359296 | tf_op jit(solution)/shard_map/all_to_all | solution.py:269
  192.3 13.8 %all-to-all-done.8 = bf16[16,144,256]{2,1,0:T(8,128)(2,1)S(1)} async-done(((bf16[16,144,256]{2,1,0:T(8,128)(2,1)}), bf16[16,144,256]{2,1,0:T(8,128)(2,1)S(1)}, u32[]{:S(2)}, u32[]{:S(2)}) %all-to-all-start.8) | async-done | bytes 1179680 | tf_op jit(solution)/shard_map/all_to_all | solution.py:269
  206.1 6.0 %all-to-all-start.7 = ((bf16[16,144,256]{2,1,0:T(8,128)(2,1)}), bf16[16,144,256]{2,1,0:T(8,128)(2,1)S(1)}, u32[]{:S(2)}, u32[]{:S(2)}) async-start(bf16[16,144,256]{2,1,0:T(8,128)(2,1)} %bitcast.49), calls=%async_computation.7 | async-start | bytes 2359296 | tf_op jit(solution)/shard_map/all_to_all | solution.py:269
  212.3 3.7 %collective-permute-start.5 = (bf16[144,256]{1,0:T(8,128)(2,1)S(1)}, bf16[144,256]{1,0:T(8,128)(2,1)S(1)}, u32[]{:S(2)}, u32[]{:S(2)}) collective-permute-start(bf16[144,256]{1,0:T(8,128)(2,1)S(1)} %reduce_sum.81), channel_id=1, source_target_pairs={{0,256},{256,0},{1,257},{257,1},{2,258},{258,2},{3,259},{259,3},{4... | collective-permute-start | bytes 221192 | tf_op jit(solution)/shard_map/ppermute | solution.py:20
  216.0 11.8 %all-to-all-done.7 = bf16[16,144,256]{2,1,0:T(8,128)(2,1)S(1)} async-done(((bf16[16,144,256]{2,1,0:T(8,128)(2,1)}), bf16[16,144,256]{2,1,0:T(8,128)(2,1)S(1)}, u32[]{:S(2)}, u32[]{:S(2)}) %all-to-all-start.7) | async-done | bytes 1179680 | tf_op jit(solution)/shard_map/all_to_all | solution.py:269
  (145 shorter events, 33.0 us)
Async XLA Ops:
  7.2 123.2 %all-gather.2.cloned.1.call-start = ((), (), s32[]{:S(2)}) async-start(), calls=%async_computation.9 | async-start | bytes 4718592 | tf_op jit(solution)/shard_map/all_gather | solution.py:176
  26.5 31.8 %all-to-all-start.1 = ((bf16[4,72,4096]{2,1,0:T(8,128)(2,1)}), bf16[4,72,4096]{2,1,0:T(8,128)(2,1)S(1)}, u32[]{:S(2)}, u32[]{:S(2)}) async-start(bf16[4,72,4096]{2,1,0:T(8,128)(2,1)} %broadcast_in_dim.20), calls=%async_computation.1 | async-start | bytes 4718592 | tf_op jit(solution)/shard_map/all_to_all | solution.py:16
  60.3 34.0 %copy-start.18 = (f32[144]{0:T(256)S(1)}, f32[144]{0:T(256)}, u32[]{:S(2)}) copy-start(f32[144]{0:T(256)} %param.17) | copy-start | bytes 1732
  60.3 34.0 %copy-start.19 = (f32[144]{0:T(256)S(1)}, f32[144]{0:T(256)}, u32[]{:S(2)}) copy-start(f32[144]{0:T(256)} %param.16) | copy-start | bytes 1732
  60.3 37.9 %copy-start.9 = (bf16[144,1024]{1,0:T(8,128)(2,1)S(1)}, bf16[144,1024]{1,0:T(8,128)(2,1)}, u32[]{:S(2)}) copy-start(bf16[144,1024]{1,0:T(8,128)(2,1)} %param.13) | copy-start | bytes 884740
  60.3 38.1 %copy-start.10 = (bf16[144,1024]{1,0:T(8,128)(2,1)S(1)}, bf16[144,1024]{1,0:T(8,128)(2,1)}, u32[]{:S(2)}) copy-start(bf16[144,1024]{1,0:T(8,128)(2,1)} %param.14) | copy-start | bytes 884740
  60.3 32.1 %all-to-all-start.2 = ((bf16[4,72,4096]{2,1,0:T(8,128)(2,1)}), bf16[4,72,4096]{2,1,0:T(8,128)(2,1)}, u32[]{:S(2)}, u32[]{:S(2)}) async-start(bf16[4,72,4096]{2,1,0:T(8,128)(2,1)} %broadcast_in_dim.22), calls=%async_computation.2 | async-start | bytes 4718592 | tf_op jit(solution)/shard_map/all_to_all | solution.py:16
  65.0 33.6 %copy-start.11 = (bf16[144,1024]{1,0:T(8,128)(2,1)S(1)}, bf16[144,1024]{1,0:T(8,128)(2,1)}, u32[]{:S(2)}) copy-start(bf16[144,1024]{1,0:T(8,128)(2,1)} %param.15) | copy-start | bytes 884740
  65.0 59.1 %collective-permute-start = (bf16[288,4096]{1,0:T(8,128)(2,1)S(1)}, bf16[288,4096]{1,0:T(8,128)(2,1)}, u32[]{:S(2)}, u32[]{:S(2)}) collective-permute-start(bf16[288,4096]{1,0:T(8,128)(2,1)S(1)} %bitcast.115), channel_id=1, source_target_pairs={{0,32},{32,0},{1,33},{33,1},{2,34},{34,2},{3,35},{35,3},{4,36},{36... | collective-permute-start | bytes 7077896 | tf_op jit(solution)/shard_map/ppermute | solution.py:20
  92.4 31.8 %collective-permute-start.1 = (bf16[288,4096]{1,0:T(8,128)(2,1)}, bf16[288,4096]{1,0:T(8,128)(2,1)}, u32[]{:S(2)}, u32[]{:S(2)}) collective-permute-start(bf16[288,4096]{1,0:T(8,128)(2,1)} %bitcast.9.policy_mine_ref), channel_id=1, source_target_pairs={{0,32},{32,0},{1,33},{33,1},{2,34},{34,2},{3,35},{35,3},{4,36},{36... | collective-permute-start | bytes 7077896 | tf_op jit(solution)/shard_map/ppermute | solution.py:20
  94.9 8.5 %all-to-all-start.4 = ((f32[4,2,144]{2,1,0:T(2,128)}), f32[4,2,144]{2,1,0:T(2,128)S(1)}, u32[]{:S(2)}, u32[]{:S(2)}) async-start(f32[4,2,144]{2,1,0:T(2,128)} %broadcast_in_dim.23), calls=%async_computation.4 | async-start | bytes 16384 | tf_op jit(solution)/shard_map/all_to_all | solution.py:16
  103.5 17.0 %all-to-all-start.3 = ((bf16[4,3,144,256]{3,2,1,0:T(8,128)(2,1)}), bf16[4,3,144,256]{3,2,1,0:T(8,128)(2,1)S(1)}, u32[]{:S(2)}, u32[]{:S(2)}) async-start(bf16[4,3,144,256]{3,2,1,0:T(8,128)(2,1)} %copy.65), calls=%async_computation.3 | async-start | bytes 1769472 | tf_op jit(solution)/shard_map/all_to_all | solution.py:187
  120.6 10.6 %copy-start.1 = (bf16[2,288,256]{2,1,0:T(8,128)(2,1)}, bf16[2,288,256]{2,1,0:T(8,128)(2,1)S(1)}, u32[]{:S(2)}) copy-start(bf16[2,288,256]{2,1,0:T(8,128)(2,1)S(1)} %pad_maximum_fusion.7.targets_ref) | copy-start | bytes 884740
  120.7 3.5 %collective-permute-start.2 = (bf16[2,288,256]{2,1,0:T(8,128)(2,1)S(1)}, bf16[2,288,256]{2,1,0:T(8,128)(2,1)S(1)}, u32[]{:S(2)}, u32[]{:S(2)}) collective-permute-start(bf16[2,288,256]{2,1,0:T(8,128)(2,1)S(1)} %pad_maximum_fusion.7.targets_ref), channel_id=1, source_target_pairs={{0,32},{32,0},{1,33},{33,1},{2,34},{34,2},{3,35},{35,3},{4,36},{36... | collective-permute-start | bytes 884744 | tf_op jit(solution)/shard_map/ppermute | solution.py:20
  131.2 32.4 %copy-start.16 = (f32[1,256]{1,0:T(1,128)S(1)}, f32[1,256]{1,0:T(1,128)}, u32[]{:S(2)}) copy-start(f32[1,256]{1,0:T(1,128)} %reshape.281.valid_ref) | copy-start | bytes 3076
  141.1 22.4 %all-to-all-start.5 = ((f32[16,4,256]{2,1,0:T(4,128)}), f32[16,4,256]{2,1,0:T(4,128)S(1)}, u32[]{:S(2)}, u32[]{:S(2)}) async-start(f32[16,4,256]{2,1,0:T(4,128)} %get-tuple-element.31), calls=%async_computation.5 | async-start | bytes 131072 | tf_op jit(solution)/shard_map/all_to_all | solution.py:205
  150.2 25.8 %collective-permute-start.3 = (bf16[2,4,256,256]{3,2,1,0:T(8,128)(2,1)}, bf16[2,4,256,256]{3,2,1,0:T(8,128)(2,1)S(1)}, u32[]{:S(2)}, u32[]{:S(2)}) collective-permute-start(bf16[2,4,256,256]{3,2,1,0:T(8,128)(2,1)} %get-tuple-element.32), channel_id=1, source_target_pairs={{0,32},{32,0},{1,33},{33,1},{2,34},{34,2},{3,35},{35,3},{4,36},{36... | collective-permute-start | bytes 3145736 | tf_op jit(solution)/shard_map/ppermute | solution.py:20
  152.3 23.7 %collective-permute-start.4 = (f32[2,288,256]{2,1,0:T(8,128)}, f32[2,288,256]{2,1,0:T(8,128)S(1)}, u32[]{:S(2)}, u32[]{:S(2)}) collective-permute-start(f32[2,288,256]{2,1,0:T(8,128)} %get-tuple-element.33), channel_id=1, source_target_pairs={{0,32},{32,0},{1,33},{33,1},{2,34},{34,2},{3,35},{35,3},{4,36},{36... | collective-permute-start | bytes 1769480 | tf_op jit(solution)/shard_map/ppermute | solution.py:20
  164.7 11.3 %all-to-all-start.6 = ((f32[32,1,776]{2,1,0:T(1,128)}), f32[32,1,776]{2,1,0:T(1,128)S(1)}, u32[]{:S(2)}, u32[]{:S(2)}) async-start(f32[32,1,776]{2,1,0:T(1,128)} %broadcast_in_dim.24), calls=%async_computation.6 | async-start | bytes 229376 | tf_op jit(solution)/shard_map/all_to_all | solution.py:16
  170.2 7.5 %copy-start.2 = (bf16[2,288,256]{2,1,0:T(8,128)(2,1)S(1)}, bf16[2,288,256]{2,1,0:T(8,128)(2,1)}, u32[]{:S(2)}) copy-start(bf16[2,288,256]{2,1,0:T(8,128)(2,1)} %copy-done.1) | copy-start | bytes 884740
  170.3 7.5 %copy-start.3 = (f32[2,288,256]{2,1,0:T(8,128)S(1)}, f32[2,288,256]{2,1,0:T(8,128)}, u32[]{:S(2)}) copy-start(f32[2,288,256]{2,1,0:T(8,128)} %get-tuple-element.33) | copy-start | bytes 1769476
  182.8 23.2 %all-to-all-start.8 = ((bf16[16,144,256]{2,1,0:T(8,128)(2,1)}), bf16[16,144,256]{2,1,0:T(8,128)(2,1)S(1)}, u32[]{:S(2)}, u32[]{:S(2)}) async-start(bf16[16,144,256]{2,1,0:T(8,128)(2,1)} %bitcast.58), calls=%async_computation.8 | async-start | bytes 2359296 | tf_op jit(solution)/shard_map/all_to_all | solution.py:269
  206.1 21.7 %all-to-all-start.7 = ((bf16[16,144,256]{2,1,0:T(8,128)(2,1)}), bf16[16,144,256]{2,1,0:T(8,128)(2,1)S(1)}, u32[]{:S(2)}, u32[]{:S(2)}) async-start(bf16[16,144,256]{2,1,0:T(8,128)(2,1)} %bitcast.49), calls=%async_computation.7 | async-start | bytes 2359296 | tf_op jit(solution)/shard_map/all_to_all | solution.py:269
  212.3 17.3 %collective-permute-start.5 = (bf16[144,256]{1,0:T(8,128)(2,1)S(1)}, bf16[144,256]{1,0:T(8,128)(2,1)S(1)}, u32[]{:S(2)}, u32[]{:S(2)}) collective-permute-start(bf16[144,256]{1,0:T(8,128)(2,1)S(1)} %reduce_sum.81), channel_id=1, source_target_pairs={{0,256},{256,0},{1,257},{257,1},{2,258},{258,2},{3,259},{259,3},{4... | collective-permute-start | bytes 221192 | tf_op jit(solution)/shard_map/ppermute | solution.py:20
  (13 other events, 34.9 us)
Sparse Core Ops, SparseCore 0:
  23.5 106.8 all-gather.1
